TPU v7x, 512 devices: a whole 4x8x8 slice. The times are simulated.
512 devices in a mesh: seq: 16 (over z, core), chan: 32 (over x, y).
Axes of the slice: x: 4, y: 8, z: 8, core: 2. Of those that a mesh axis runs over, the one named last changes fastest.
Arguments:
- tokens: bfloat16 [4096, 4096], P('seq', 'chan'), may hold values from -6 to 6
- w_in: bfloat16 [4096, 3, 4096], P(None, None, 'chan'), may hold values from -0.09375 to 0.09375
- filters: bfloat16 [256, 4096], P('chan'), may hold values from -0.09375 to 0.09375
- skip: float32 [4096], P('chan'), may hold values from 0.25 to 1.5
- w_out: bfloat16 [4096, 4096], P(None, 'chan'), may hold values from -0.09375 to 0.09375
Outputs:
- mixed: bfloat16 [4096, 4096], P('seq', 'chan')
All inputs are finite; a program needn't handle non-finite values.
Results may differ from a plain program's by a relative error of at most 0.015.
Values may be sent and summed in bfloat16 or wider, within the bound.
No kernel may reach another device: no remote copies, remote signals or barrier semaphores. Data moves between devices by JAX's collectives and lax.ppermute only.
A program may use at most 64 MiB of HBM per device.

v0:
```python
import math

import jax
import jax.numpy as jnp
from jax import lax
from jax.sharding import PartitionSpec as P


def toeplitz(padded, lead, offset, rows, cols):
    span = rows + cols
    segment = lax.dynamic_slice_in_dim(padded, lead + offset - cols + 1, span, 1)
    rolled = jnp.concatenate([segment[:, cols - 1 :], segment[:, : cols - 1]], axis=1)
    flat = jnp.tile(rolled, (1, cols))[:, : cols * (span - 1)]
    return flat.reshape(padded.shape[0], cols, span - 1)[:, :, :rows]


def apply_groups(matrix, values):
    groups = matrix.shape[0]
    grouped = values.reshape(values.shape[0], groups, -1)
    result = jnp.einsum("jgc,gji->gci", grouped, matrix, preferred_element_type=jnp.float32)
    return result.reshape(values.shape[1], matrix.shape[2]).T


def shards(tokens, w_in, filters, skip, w_out):
    block_len = tokens.shape[0]
    chans = w_out.shape[1]
    w_flat = w_in.reshape(w_in.shape[0], 3 * chans)
    rows = w_flat
    qkv = jnp.dot(
        lax.all_gather(tokens, "chan", axis=1, tiled=True), rows, preferred_element_type=jnp.float32
    )
    qkv = qkv.astype(jnp.bfloat16).reshape(block_len, 3, chans)
    query = qkv[:, 0]
    source = (qkv[:, 1].astype(jnp.float32) * qkv[:, 2].astype(jnp.float32)).astype(jnp.bfloat16)
    seq_rank = lax.axis_index("seq")
    lead = 2 * block_len
    row_first = seq_rank * block_len
    padded = jnp.pad(filters, ((0, 0), (lead, 1)))
    piece = lax.all_gather(source, "seq", axis=0, tiled=True)
    width = math.gcd(piece.shape[0], block_len)

    def visit(turn, carry):
        col_first = turn * width
        sub_block = lax.dynamic_slice_in_dim(piece, turn * width, width, 0)

        def contribute(acc):
            matrix = toeplitz(padded, lead, row_first - col_first, block_len, width)
            return acc + apply_groups(matrix, sub_block)

        return lax.cond(col_first < row_first + block_len, contribute, lambda acc: acc, carry)

    conv = lax.fori_loop(
        0, piece.shape[0] // width, visit, jnp.zeros((block_len, chans), jnp.float32)
    )
    gated = (
        query.astype(jnp.float32) * (conv + skip[None, :] * source.astype(jnp.float32))
    ).astype(jnp.bfloat16)
    rows = w_out
    mixed = jnp.dot(
        lax.all_gather(gated, "chan", axis=1, tiled=True), rows, preferred_element_type=jnp.float32
    )
    return mixed.astype(jnp.bfloat16)


def solution(mesh):
    in_specs = (
        P("seq", "chan"),
        P(None, None, "chan"),
        P("chan", None),
        P("chan"),
        P(None, "chan"),
    )
    out_specs = P("seq", "chan")
    return jax.shard_map(shards, mesh=mesh, in_specs=in_specs, out_specs=out_specs, check_vma=False)
```

profile of v0, /device:TPU:1, one launch (start us, length us, event | category | flops | bytes accessed | tf_op | source)
XLA Modules:
  0.0 407.7 jit_solution(13379084503499515155)
XLA Ops:
  6.5 0.7 all-gather.5.cloned.1.call-update
  7.3 4.7 %copy.9 = bf16[4096,3,128]{0,2,1:T(8,128)(2,1)} copy(bf16[4096,3,128]{2,0,1:T(8,128)(2,1)} %param.10) | data formatting | bytes 6291456 | tf_op args[1]
  12.0 81.1 %all-gather.5.cloned.1.call-done = bf16[256,4096]{1,0:T(8,128)(2,1)} async-done(((bf16[256,128]{1,0:T(8,128)(2,1)}), bf16[256,4096]{1,0:T(8,128)(2,1)}) %all-gather.5.cloned.1.call-update) | async-done | bytes 2097168 | tf_op jit(solution)/shard_map/all_gather | solution.py:30
  93.1 3.8 convolution_convert_fusion
  96.9 0.1 copy.10
  97.0 0.6 multiply_convert_fusion
  97.7 0.0 all-gather.7.cloned.1.call-start
  97.8 43.9 %all-gather.9.cloned.1.call-done = bf16[4096,1,128]{0,2,1:T(8,128)(2,1)} async-done(((bf16[256,1,128]{0,2,1:T(8,128)(2,1)}), bf16[4096,1,128]{0,2,1:T(8,128)(2,1)}) %all-gather.9.cloned.1.call-update) | async-done | bytes 1048592 | tf_op jit(solution)/shard_map/all_gather | solution.py:39
  141.8 22.9 %while.17 = (s32[]{:T(128)}, f32[256,128]{0,1:T(8,128)S(1)}, s32[]{:T(128)}, bf16[4096,128]{0,1:T(8,128)(2,1)}, s32[]{:T(128)}, /*index=5*/bf16[8,4609]{1,0:T(8,128)(2,1)S(1)}, s32[]{:T(128)}, s32[]{:T(128)}) while((s32[]{:T(128)}, f32[256,128]{0,1:T(8,128)S(1)}, s32[]{:T(128)}, bf16[4096,128]{0,1:T(8,128)(2,1)}, s32[]{:T(128)}, ...), condition=%wide.region_3.4_spmd, body=%wide.region_0.3_spmd.sunk | while | flops 16826380 | bytes 16466195 | solution.py:52
  141.8 11.2 %conditional.2 = (f32[256,128]{0,1:T(8,128)S(1)}) conditional(s32[]{:T(128)} %convert_element_type.67, f32[256,128]{0,1:T(8,128)S(1)} %get-tuple-element.249, (s32[]{:T(128)}, bf16[4096,128]{0,1:T(8,128)(2,1)}, s32[]{:T(128)}, bf16[8,4609]{1,0:T(8,128)(2,1)S(1)}, f32[256,128]{0,1:T(8,128)S(1)}) %tuple.50), branch_computations={%region_1.1_spmd, %region_2.2_spmd} | conditional | flops 16826376 | bytes 16466044 | solution.py:50
  141.8 0.1 constant_dynamic-slice_fusion
  141.9 0.1 constant_dynamic-slice_fusion.1
  142.0 0.1 pad_maximum_fusion
  142.0 0.1 tile.4
  142.2 0.1 slice.32
  142.3 4.4 %reshape.37 = bf16[1046528]{0:T(1024)(128)(2,1)} reshape(bf16[8,130816]{1,0:T(8,128)(2,1)S(1)} %slice.32) | data formatting | bytes 4186112 | tf_op jit(solution)/shard_map/while/body/eval_jaxpr/cond
  146.8 5.0 %reshape.28 = bf16[8,256,511]{2,1,0:T(8,128)(2,1)S(1)} reshape(bf16[1046528]{0:T(1024)(128)(2,1)} %reshape.37) | data formatting | bytes 4186112 | tf_op jit(solution)/shard_map/while/body/eval_jaxpr/cond/branch_1_fun/reshape | solution.py:14
  151.8 0.8 constant_dynamic-slice_fusion.2
  152.7 0.2 fusion
  153.0 11.2 %conditional.2 = (f32[256,128]{0,1:T(8,128)S(1)}) conditional(s32[]{:T(128)} %convert_element_type.67, f32[256,128]{0,1:T(8,128)S(1)} %get-tuple-element.249, (s32[]{:T(128)}, bf16[4096,128]{0,1:T(8,128)(2,1)}, s32[]{:T(128)}, bf16[8,4609]{1,0:T(8,128)(2,1)S(1)}, f32[256,128]{0,1:T(8,128)S(1)}) %tuple.50), branch_computations={%region_1.1_spmd, %region_2.2_spmd} | conditional | flops 16826376 | bytes 16466044 | solution.py:50
  153.0 0.1 constant_dynamic-slice_fusion
  153.1 0.1 constant_dynamic-slice_fusion.1
  153.1 0.1 pad_maximum_fusion
  153.2 0.1 tile.4
  153.4 0.1 slice.32
  153.5 4.4 %reshape.37 = bf16[1046528]{0:T(1024)(128)(2,1)} reshape(bf16[8,130816]{1,0:T(8,128)(2,1)S(1)} %slice.32) | data formatting | bytes 4186112 | tf_op jit(solution)/shard_map/while/body/eval_jaxpr/cond
  158.0 5.0 %reshape.28 = bf16[8,256,511]{2,1,0:T(8,128)(2,1)S(1)} reshape(bf16[1046528]{0:T(1024)(128)(2,1)} %reshape.37) | data formatting | bytes 4186112 | tf_op jit(solution)/shard_map/while/body/eval_jaxpr/cond/branch_1_fun/reshape | solution.py:14
  163.0 0.8 constant_dynamic-slice_fusion.2
  163.8 0.2 fusion
  164.7 0.7 fusion.4
  165.5 232.7 %all-gather.7.cloned.1.call-done = bf16[256,4096]{0,1:T(8,128)(2,1)} async-done(((bf16[256,128]{0,1:T(8,128)(2,1)}), bf16[256,4096]{0,1:T(8,128)(2,1)}) %all-gather.7.cloned.1.call-update) | async-done | bytes 2097168 | tf_op jit(solution)/shard_map/all_gather | solution.py:60
  398.2 3.0 convolution_convert_fusion.1
  (28 shorter events, 0.3 us)
Async XLA Ops:
  6.5 391.6 %copy-start = (bf16[4096,128]{1,0:T(8,128)(2,1)S(1)}, bf16[4096,128]{1,0:T(8,128)(2,1)}, u32[]{:S(2)}) copy-start(bf16[4096,128]{1,0:T(8,128)(2,1)} %param.13) | copy-start | bytes 3145732
  6.5 86.5 %all-gather.5.cloned.1.call-start = ((), (), s32[]{:S(2)}) async-start(), calls=%async_computation | async-start | bytes 2162688 | tf_op jit(solution)/shard_map/all_gather | solution.py:30
  7.3 134.5 %all-gather.9.cloned.1.call-start = ((), (), s32[]{:S(2)}) async-start(), calls=%async_computation.2 | async-start | bytes 1114112 | tf_op jit(solution)/shard_map/all_gather | solution.py:39
  93.1 4.7 %copy-start.1 = (bf16[8,4096]{1,0:T(8,128)(2,1)S(1)}, bf16[8,4096]{1,0:T(8,128)(2,1)}, u32[]{:S(2)}) copy-start(bf16[8,4096]{1,0:T(8,128)(2,1)} %param.11) | copy-start | bytes 196612
  97.7 300.5 %all-gather.7.cloned.1.call-start = ((), (), s32[]{:S(2)}) async-start(), calls=%async_computation.1 | async-start | bytes 2162688 | tf_op jit(solution)/shard_map/all_gather | solution.py:60
  141.7 23.0 %copy-start.2 = (f32[128]{0:T(128)S(1)}, f32[128]{0:T(128)}, u32[]{:S(2)}) copy-start(f32[128]{0:T(128)} %param.12) | copy-start | bytes 1540
Sparse Core Ops, SparseCore 0:
  10.4 82.6 all-gather.4
  97.8 43.8 all-gather.8
  165.6 232.5 all-gather.6
where the time goes:
time: 411 us; the launch traced here: 408 us
  waiting for transfers between devices  358 us (87%)
  local copies, waits for them, and re-layouts  26.4 us (6%)
  between operations  13.2 us (3%)
  matrix products  7.28 us (2%)
    all_gather x1, waiting for transfers between devices, shards(): lax.all_gather(gated, 'chan', axis=1, tiled=True)  233 us
    all_gather x1, waiting for transfers between devices, shards(): lax.all_gather(tokens, 'chan', axis=1, tiled=True)  81.1 us
    all_gather x1, waiting for transfers between devices, shards(): piece = lax.all_gather(source, 'seq', axis=0, tiled=True)  43.9 us
    reshape x2, local copies, waits for them, and re-layouts, toeplitz(): return flat.reshape(padded.shape[0], cols, span - 1)[:, :, :rows]  10 us
    cond x2, local copies, waits for them, and re-layouts  8.89 us
  transfers between devices with their start and end apart: 3, of which 3 were waited for; matrix products, arithmetic and copies ran while one was open for 1% of the time, Pallas kernels for 0%

commit v1 on v0

v1 whole, which is shorter than its diff:
```python
import jax
import jax.numpy as jnp
from jax import lax
from jax.experimental import pallas as pl
from jax.experimental.pallas import tpu as pltpu
from jax.sharding import Mesh
from jax.sharding import PartitionSpec as P

GROUP = 16
LANES = 128


def vmem(*shape_and_map):
    return pl.BlockSpec(*shape_and_map, memory_space=pltpu.VMEM)


def spread(block, axis, size):
    copies = jnp.broadcast_to(block[None], (size,) + block.shape)
    return lax.all_to_all(copies, axis, 0, 0, tiled=True)


def project_kernel(x_ref, w_ref, out_ref, acc_ref):
    step = pl.program_id(0)
    left = jnp.concatenate([x_ref[i] for i in range(x_ref.shape[0])], axis=1)
    right = jnp.concatenate([w_ref[0], w_ref[1], w_ref[2]], axis=1)
    part = jnp.dot(left, right, preferred_element_type=jnp.float32)

    @pl.when(step == 0)
    def _():
        acc_ref[...] = part

    @pl.when(step > 0)
    def _():
        acc_ref[...] += part

    @pl.when(step == pl.num_programs(0) - 1)
    def _():
        chans = w_ref.shape[2]
        query, key, value = (
            acc_ref[:, i * chans : (i + 1) * chans].astype(jnp.bfloat16).astype(jnp.float32) for i in range(3)
        )
        source = (key * value).T.astype(jnp.bfloat16)
        query = query.T.astype(jnp.bfloat16)
        groups = chans // GROUP
        out_ref[:, :GROUP, :] = source.reshape(groups, GROUP, -1)
        out_ref[:, GROUP:, :] = query.reshape(groups, GROUP, -1)


def project(x, w):
    slabs, tokens, depth = x.shape
    chans = w.shape[2]
    each = slabs // 4
    return pl.pallas_call(
        project_kernel,
        grid=(4,),
        in_specs=[
            vmem((each, tokens, depth), lambda s: (s, 0, 0)),
            vmem((3, each * depth, chans), lambda s: (0, s, 0)),
        ],
        out_specs=vmem((chans // GROUP, 2 * GROUP, tokens), lambda s: (0, 0, 0)),
        out_shape=jax.ShapeDtypeStruct((chans // GROUP, 2 * GROUP, tokens), jnp.bfloat16),
        scratch_shapes=[pltpu.VMEM((tokens, 3 * chans), jnp.float32)],
        compiler_params=pltpu.CompilerParams(vmem_limit_bytes=40 * 2**20),
        name="project",
    )(x, w)


def conv_kernel(pieces_ref, filters_ref, skip_ref, out_ref, shifted_ref, strip_ref, skip_rows_ref, acc_ref):
    core, group = lax.axis_index("core"), lax.axis_index("z")
    blocks, _, block = pieces_ref.shape[1:]
    rows = blocks * GROUP
    own = pieces_ref[core]
    source = own[:, :GROUP, :].reshape(rows, block)
    query = own[:, GROUP:, :].reshape(rows, block)
    other = pieces_ref[1 - core][:, :GROUP, :].reshape(rows, block)
    shifted_ref[:GROUP, :] = jnp.zeros((GROUP, block), jnp.bfloat16)
    shifted_ref[GROUP:, :] = other
    other = shifted_ref[pl.ds(pl.multiple_of(core * GROUP, GROUP), rows), :]
    left = jnp.concatenate([source, other], axis=1)

    all_taps = filters_ref[...].astype(jnp.float32)
    mine = lax.broadcasted_iota(jnp.int32, all_taps.shape, 0) == group
    taps = jnp.sum(jnp.where(mine, all_taps, 0.0), axis=0, keepdims=True)
    length = taps.shape[1]
    padded = jnp.concatenate([jnp.zeros((1, LANES), jnp.float32), taps], axis=1)
    rolled = pltpu.roll(jnp.broadcast_to(padded, (LANES, LANES + length)), 0, 1, stride=1, stride_axis=0)
    strip_ref[:, :LANES] = jnp.zeros((LANES, LANES), jnp.bfloat16)
    strip_ref[:, LANES:] = rolled[:, LANES:].astype(jnp.bfloat16)

    for e in range(blocks):
        first = 2 * e * block
        right = jnp.concatenate(
            [
                strip_ref[:, at : at + block]
                for at in (first + LANES, first, first + block + LANES, first + block)
            ],
            axis=0,
        )
        height = rows - e * GROUP
        part = jnp.dot(left[:height], right, preferred_element_type=jnp.float32)
        if e == 0:
            acc_ref[...] = part
        else:
            acc_ref[e * GROUP :, :] += part

    skip_rows_ref[...] = jnp.broadcast_to(skip_ref[...], (LANES, LANES)).T
    skip = skip_rows_ref[pl.ds(pl.multiple_of(group * GROUP, GROUP), GROUP), :]
    skip = jnp.concatenate([skip] * (block // LANES), axis=1)
    skip = jnp.concatenate([skip] * blocks, axis=0)
    gated = query.astype(jnp.float32) * (acc_ref[...] + skip * source.astype(jnp.float32))
    out_ref[...] = gated.astype(jnp.bfloat16).reshape(out_ref.shape)


def convolve(pieces, filters, skip):
    _, blocks, _, block = pieces.shape
    rows = blocks * GROUP
    return pl.pallas_call(
        conv_kernel,
        in_specs=[vmem(), vmem(), vmem()],
        out_specs=vmem(),
        out_shape=jax.ShapeDtypeStruct((blocks, GROUP, block), jnp.bfloat16),
        scratch_shapes=[
            pltpu.VMEM((rows + GROUP, block), jnp.bfloat16),
            pltpu.VMEM((LANES, LANES + filters.shape[1]), jnp.bfloat16),
            pltpu.VMEM((LANES, LANES), jnp.float32),
            pltpu.VMEM((rows, block), jnp.float32),
        ],
        compiler_params=pltpu.CompilerParams(vmem_limit_bytes=40 * 2**20),
        name="convolve",
    )(pieces, filters, skip)


def mix_kernel(g_ref, w_ref, out_ref, acc_ref):
    step = pl.program_id(0)
    left = g_ref[...].reshape(-1, g_ref.shape[2])
    part = lax.dot_general(left, w_ref[...], (((0,), (0,)), ((), ())), preferred_element_type=jnp.float32)

    @pl.when(step == 0)
    def _():
        acc_ref[...] = part

    @pl.when(step > 0)
    def _():
        acc_ref[...] += part

    @pl.when(step == pl.num_programs(0) - 1)
    def _():
        out_ref[...] = acc_ref[...].astype(jnp.bfloat16)


def mix(gated, w):
    slabs, depth, tokens = gated.shape
    chans = w.shape[1]
    each = slabs // 4
    return pl.pallas_call(
        mix_kernel,
        grid=(4,),
        in_specs=[
            vmem((each, depth, tokens), lambda s: (s, 0, 0)),
            vmem((each * depth, chans), lambda s: (s, 0)),
        ],
        out_specs=vmem((tokens, chans), lambda s: (0, 0)),
        out_shape=jax.ShapeDtypeStruct((tokens, chans), jnp.bfloat16),
        scratch_shapes=[pltpu.VMEM((tokens, chans), jnp.float32)],
        compiler_params=pltpu.CompilerParams(vmem_limit_bytes=40 * 2**20),
        name="mix",
    )(gated, w)


def shards(tokens, w_in, filters, skip, w_out):
    def over_chan(block):
        rows = spread(block, "y", 8)
        return spread(rows, "x", 4).reshape((32,) + block.shape)

    pieces = project(over_chan(tokens), w_in.transpose(1, 0, 2))
    pieces = lax.all_to_all(pieces, "z", 0, 0, tiled=True)
    gated = convolve(lax.all_gather(pieces, "core", axis=0), filters, skip.reshape(1, -1))
    gated = lax.all_to_all(gated, "z", 0, 0, tiled=True)
    return mix(over_chan(gated.reshape(-1, gated.shape[2])), w_out)


def solution(mesh):
    fine = Mesh(mesh.devices.reshape(8, 2, 4, 8), ("z", "core", "x", "y"))
    seq, chan = ("z", "core"), ("x", "y")
    in_specs = (P(seq, chan), P(None, None, chan), P(chan, None), P(chan), P(None, chan))
    return jax.shard_map(shards, mesh=fine, in_specs=in_specs, out_specs=P(seq, chan), check_vma=False)
```

time: 411 us -> 137 us (0.33)
  waiting for transfers between devices: 358 us -> 0 us
  blocking collectives: 0 us -> 127 us
  local copies, waits for them, and re-layouts: 26.4 us -> 1.67 us
  between operations: 13.2 us -> 0.05 us
  matrix products: 7.28 us -> 0 us
  Pallas kernels: 0 us -> 4.97 us
    all_gather x3 -> x0, waiting for transfers between devices: 358 us -> none  [the longest x1 233 us: shards(): lax.all_gather(gated, 'chan', axis=1, tiled=True)]
    all_to_all x0 -> x6, blocking collectives: none -> 120 us  [the longest x4 93.2 us: spread(): return lax.all_to_all(copies, axis, 0, 0, tiled=True)]
    reshape x2 -> x0, local copies, waits for them, and re-layouts: 10 us -> none  [toeplitz(): return flat.reshape(padded.shape[0], cols, span - 1)[:, :, :rows]]
    cond x2 -> x0, local copies, waits for them, and re-layouts: 8.89 us -> none
    dot_general x4 -> x0, matrix products: 7.28 us -> none  [the longest x1 3.82 us: shards(): jnp.dot(lax.all_gather(tokens, 'chan', axis=1, tiled=True), rows, preferr...]
    all_gather x0 -> x1, blocking collectives: none -> 7 us  [shards(): lax.all_gather(pieces, 'core', axis=0)]
    pallas_call x0 -> x3, Pallas kernels: none -> 4.97 us  [the longest x1 2.24 us: project(): pl.pallas_call(project_kernel, grid=(4,), in_specs=[vmem((each, tokens, d...]
    unnamed x7 -> x8, local copies, waits for them, and re-layouts: 4.69 us -> 0.02 us
  transfers between devices with their start and end apart: 3 -> 0, of which waited for: 3 -> 0; matrix products, arithmetic and copies ran while one was open for 1% -> 0% of each run, Pallas kernels for 0% -> 0%
where the time goes in v1:
time: 137 us; the launch traced here: 134 us
  blocking collectives  127 us (93%)
  Pallas kernels  4.97 us (4%)
  local copies, waits for them, and re-layouts  1.67 us (1%)
    all_to_all x4, blocking collectives, spread(): return lax.all_to_all(copies, axis, 0, 0, tiled=True)  93.2 us
    all_to_all x1, blocking collectives, shards(): pieces = lax.all_to_all(pieces, 'z', 0, 0, tiled=True)  17.8 us
    all_to_all x1, blocking collectives, shards(): gated = lax.all_to_all(gated, 'z', 0, 0, tiled=True)  9.51 us
    all_gather x1, blocking collectives, shards(): lax.all_gather(pieces, 'core', axis=0)  7 us

profile of v1, /device:TPU:1, one launch (start us, length us, event | category | flops | bytes accessed | tf_op | source)
XLA Modules:
  0.0 134.2 jit_solution(14218446408628420791)
XLA Ops:
  0.0 0.9 broadcast_in_dim.10
  0.9 22.2 %all_to_all.30 = bf16[8,256,128]{2,1,0:T(8,128)(2,1)S(1)} all-to-all(bf16[8,256,128]{2,1,0:T(8,128)(2,1)S(1)} %broadcast_in_dim.10), channel_id=1, replica_groups=mesh['z'=8,'core'=2,'x'=4,'y'=8] {'y'}, dimensions={0} | all-to-all | bytes 1048576 | tf_op jit(solution)/shard_map/all_to_all | solution.py:19
  23.1 0.5 broadcast_in_dim.11
  23.6 0.0 copy-start
  23.6 28.7 %all_to_all.31 = bf16[4,8,256,128]{3,2,1,0:T(8,128)(2,1)S(1)} all-to-all(bf16[4,8,256,128]{3,2,1,0:T(8,128)(2,1)S(1)} %broadcast_in_dim.11), channel_id=1, replica_groups=mesh['z'=8,'core'=2,'x'=4,'y'=8] {'x'}, dimensions={0} | all-to-all | bytes 4194304 | tf_op jit(solution)/shard_map/all_to_all | solution.py:19
  52.2 0.0 copy-done
  52.2 0.0 copy-start.2
  52.3 0.0 copy-start.3
  52.3 2.2 %project.1 = bf16[8,32,256]{2,1,0:T(8,128)(2,1)S(1)} custom-call(bf16[32,256,128]{2,1,0:T(8,128)(2,1)S(1)} %bitcast.7, bf16[3,4096,128]{2,1,0:T(8,128)(2,1)S(1)} %bitcast.8), custom_call_target="tpu_custom_call" | custom-call | tf_op jit(solution)/shard_map/project/pallas_call | solution.py:53
  54.5 17.8 %all_to_all.32 = bf16[8,32,256]{2,1,0:T(8,128)(2,1)S(1)} all-to-all(bf16[8,32,256]{2,1,0:T(8,128)(2,1)S(1)} %project.1), channel_id=1, replica_groups=mesh['z'=8,'core'=2,'x'=4,'y'=8] {'z'}, dimensions={0} | all-to-all | bytes 262144 | tf_op jit(solution)/shard_map/all_to_all | solution.py:176
  72.3 7.0 %all-gather = bf16[16,32,256]{2,1,0:T(8,128)(2,1)S(1)} all-gather(bf16[8,32,256]{2,1,0:T(8,128)(2,1)S(1)} %all_to_all.32), channel_id=2, replica_groups=mesh['z'=8,'core'=2,'x'=4,'y'=8] {'core'}, dimensions={0}, use_global_device_ids=true | all-gather | bytes 393216 | tf_op jit(solution)/shard_map/all_gather | solution.py:177
  79.3 0.0 copy-done.2
  79.3 0.0 copy-done.3
  79.3 0.7 convolve.1
  79.9 9.5 %all_to_all.33 = bf16[8,16,256]{2,1,0:T(8,128)(2,1)S(1)} all-to-all(bf16[8,16,256]{2,1,0:T(8,128)(2,1)S(1)} %convolve.1), channel_id=1, replica_groups=mesh['z'=8,'core'=2,'x'=4,'y'=8] {'z'}, dimensions={0} | all-to-all | bytes 131072 | tf_op jit(solution)/shard_map/all_to_all | solution.py:178
  89.5 17.1 %all_to_all.34 = bf16[8,128,256]{2,1,0:T(8,128)(2,1)S(1)} all-to-all(bf16[8,128,256]{2,1,0:T(8,128)(2,1)S(1)} %broadcast_in_dim.13), channel_id=1, replica_groups=mesh['z'=8,'core'=2,'x'=4,'y'=8] {'y'}, dimensions={0} | all-to-all | bytes 1048576 | tf_op jit(solution)/shard_map/all_to_all | solution.py:19
  106.6 0.2 broadcast_in_dim.14
  106.9 0.0 copy-start.1
  106.9 25.2 %all_to_all.35 = bf16[4,8,128,256]{3,2,1,0:T(8,128)(2,1)S(1)} all-to-all(bf16[4,8,128,256]{3,2,1,0:T(8,128)(2,1)S(1)} %broadcast_in_dim.14), channel_id=1, replica_groups=mesh['z'=8,'core'=2,'x'=4,'y'=8] {'x'}, dimensions={0} | all-to-all | bytes 4194304 | tf_op jit(solution)/shard_map/all_to_all | solution.py:19
  132.1 0.0 copy-done.1
  132.1 2.1 %mix.1 = bf16[256,128]{1,0:T(8,128)(2,1)} custom-call(bf16[32,128,256]{2,1,0:T(8,128)(2,1)S(1)} %bitcast.6, bf16[4096,128]{1,0:T(8,128)(2,1)S(1)} %copy-done.1), custom_call_target="tpu_custom_call" | custom-call | tf_op jit(solution)/shard_map/mix/pallas_call | solution.py:155
  (1 shorter events, 0.0 us)
Async XLA Ops:
  23.6 28.7 %copy-start = (bf16[4096,3,128]{2,0,1:T(8,128)(2,1)S(1)}, bf16[4096,3,128]{2,0,1:T(8,128)(2,1)}, u32[]{:S(2)}) copy-start(bf16[4096,3,128]{2,0,1:T(8,128)(2,1)} %param.6) | copy-start | bytes 9437188
  52.2 27.0 %copy-start.2 = (bf16[8,4096]{1,0:T(8,128)(2,1)S(1)}, bf16[8,4096]{1,0:T(8,128)(2,1)}, u32[]{:S(2)}) copy-start(bf16[8,4096]{1,0:T(8,128)(2,1)} %filters_ref.1) | copy-start | bytes 196612
  52.3 27.0 %copy-start.3 = (f32[128]{0:T(128)S(1)}, f32[128]{0:T(128)}, u32[]{:S(2)}) copy-start(f32[128]{0:T(128)} %param.8) | copy-start | bytes 1540
  106.9 25.2 %copy-start.1 = (bf16[4096,128]{1,0:T(8,128)(2,1)S(1)}, bf16[4096,128]{1,0:T(8,128)(2,1)}, u32[]{:S(2)}) copy-start(bf16[4096,128]{1,0:T(8,128)(2,1)} %w_ref.1) | copy-start | bytes 3145732

commit v2 on v1

v2 whole, which is shorter than its diff:
```python
import jax
import jax.numpy as jnp
from jax import lax
from jax.experimental import pallas as pl
from jax.experimental.pallas import tpu as pltpu
from jax.sharding import Mesh
from jax.sharding import PartitionSpec as P

GROUP = 16
LANES = 128
PARAMS = pltpu.CompilerParams(vmem_limit_bytes=40 * 2**20)


def vmem(*shape_and_map):
    return pl.BlockSpec(*shape_and_map, memory_space=pltpu.VMEM)


def copies(block, count):
    return jnp.broadcast_to(block[None], (count,) + block.shape)


def over_chan(blocks):
    rows = lax.all_to_all(blocks, "y_far", 0, 0, tiled=True)
    whole = lax.all_to_all(copies(rows, 8), ("x", "y_near"), 0, 0, tiled=True)
    return whole.reshape((4, 2) + rows.shape)


def project_kernel(x_ref, w_ref, out_ref):
    steps, near, far, tokens, depth = x_ref.shape
    chans = w_ref.shape[2]
    span = near * far * depth
    acc = None
    for step in range(steps):
        left = jnp.concatenate([x_ref[step, j, i] for i in range(far) for j in range(near)], axis=1)
        right = jnp.concatenate([w_ref[i, step * span : (step + 1) * span] for i in range(3)], axis=1)
        part = jnp.dot(left, right, preferred_element_type=jnp.float32)
        acc = part if acc is None else acc + part
    query, key, value = (
        acc[:, i * chans : (i + 1) * chans].astype(jnp.bfloat16).astype(jnp.float32) for i in range(3)
    )
    groups = chans // GROUP
    out_ref[:, :GROUP, :] = (key * value).T.astype(jnp.bfloat16).reshape(groups, GROUP, -1)
    out_ref[:, GROUP:, :] = query.T.astype(jnp.bfloat16).reshape(groups, GROUP, -1)


def project(x, w):
    tokens, chans = x.shape[3], w.shape[2]
    return pl.pallas_call(
        project_kernel,
        in_specs=[vmem(), vmem()],
        out_specs=vmem(),
        out_shape=jax.ShapeDtypeStruct((chans // GROUP, 2 * GROUP, tokens), jnp.bfloat16),
        compiler_params=PARAMS,
        name="project",
    )(x, w)


def conv_kernel(pieces_ref, filters_ref, skip_ref, out_ref, shifted_ref, strip_ref, skip_rows_ref, acc_ref):
    core, group = lax.axis_index("core"), lax.axis_index("z")
    blocks, _, block = pieces_ref.shape[1:]
    rows = blocks * GROUP
    own = pieces_ref[core]
    source = own[:, :GROUP, :].reshape(rows, block)
    query = own[:, GROUP:, :].reshape(rows, block)
    other = pieces_ref[1 - core][:, :GROUP, :].reshape(rows, block)
    shifted_ref[:GROUP, :] = jnp.zeros((GROUP, block), jnp.bfloat16)
    shifted_ref[GROUP:, :] = other
    other = shifted_ref[pl.ds(pl.multiple_of(core * GROUP, GROUP), rows), :]
    left = jnp.concatenate([source, other], axis=1)

    all_taps = filters_ref[...].astype(jnp.float32)
    mine = lax.broadcasted_iota(jnp.int32, all_taps.shape, 0) == group
    taps = jnp.sum(jnp.where(mine, all_taps, 0.0), axis=0, keepdims=True)
    length = taps.shape[1]
    padded = jnp.concatenate([jnp.zeros((1, LANES), jnp.float32), taps], axis=1)
    rolled = pltpu.roll(jnp.broadcast_to(padded, (LANES, LANES + length)), 0, 1, stride=1, stride_axis=0)
    strip_ref[:, :LANES] = jnp.zeros((LANES, LANES), jnp.bfloat16)
    strip_ref[:, LANES:] = rolled[:, LANES:].astype(jnp.bfloat16)

    for e in range(blocks):
        first = 2 * e * block
        right = jnp.concatenate(
            [
                strip_ref[:, at : at + block]
                for at in (first + LANES, first, first + block + LANES, first + block)
            ],
            axis=0,
        )
        height = rows - e * GROUP
        part = jnp.dot(left[:height], right, preferred_element_type=jnp.float32)
        if e == 0:
            acc_ref[...] = part
        else:
            acc_ref[e * GROUP :, :] += part

    skip_rows_ref[...] = jnp.broadcast_to(skip_ref[...], (LANES, LANES)).T
    skip = skip_rows_ref[pl.ds(pl.multiple_of(group * GROUP, GROUP), GROUP), :]
    skip = jnp.concatenate([skip] * (block // LANES), axis=1)
    skip = jnp.concatenate([skip] * blocks, axis=0)
    gated = query.astype(jnp.float32) * (acc_ref[...] + skip * source.astype(jnp.float32))
    out_ref[...] = gated.astype(jnp.bfloat16).reshape(out_ref.shape)


def convolve(pieces, filters, skip):
    _, blocks, _, block = pieces.shape
    rows = blocks * GROUP
    return pl.pallas_call(
        conv_kernel,
        in_specs=[vmem(), vmem(), vmem()],
        out_specs=vmem(),
        out_shape=jax.ShapeDtypeStruct((blocks, GROUP, block), jnp.bfloat16),
        scratch_shapes=[
            pltpu.VMEM((rows + GROUP, block), jnp.bfloat16),
            pltpu.VMEM((LANES, LANES + filters.shape[1]), jnp.bfloat16),
            pltpu.VMEM((LANES, LANES), jnp.float32),
            pltpu.VMEM((rows, block), jnp.float32),
        ],
        compiler_params=PARAMS,
        name="convolve",
    )(pieces, filters, skip)


def turn_kernel(g_ref, out_ref):
    turned = g_ref[...].astype(jnp.float32).reshape(-1, g_ref.shape[2]).T.astype(jnp.bfloat16)
    for i in range(out_ref.shape[0]):
        out_ref[i] = turned


def turn(gated, copies):
    sources, rows, tokens = gated.shape
    return pl.pallas_call(
        turn_kernel,
        in_specs=[vmem()],
        out_specs=vmem(),
        out_shape=jax.ShapeDtypeStruct((copies, tokens, sources * rows), jnp.bfloat16),
        compiler_params=PARAMS,
        name="turn",
    )(gated)


def mix_kernel(g_ref, w_ref, out_ref):
    steps, near, far, tokens, depth = g_ref.shape
    span = near * far * depth
    acc = None
    for step in range(steps):
        left = jnp.concatenate([g_ref[step, j, i] for i in range(far) for j in range(near)], axis=1)
        part = jnp.dot(left, w_ref[step * span : (step + 1) * span], preferred_element_type=jnp.float32)
        acc = part if acc is None else acc + part
    out_ref[...] = acc.astype(jnp.bfloat16)


def mix(gated, w):
    return pl.pallas_call(
        mix_kernel,
        in_specs=[vmem(), vmem()],
        out_specs=vmem(),
        out_shape=jax.ShapeDtypeStruct((gated.shape[3], w.shape[1]), jnp.bfloat16),
        compiler_params=PARAMS,
        name="mix",
    )(gated, w)


def shards(tokens, w_in, filters, skip, w_out):
    pieces = project(over_chan(copies(tokens, 4)), w_in.transpose(1, 0, 2))
    pieces = lax.all_to_all(pieces, "z", 0, 0, tiled=True)
    gated = convolve(lax.all_gather(pieces, "core", axis=0), filters, skip.reshape(1, -1))
    gated = lax.all_to_all(gated, "z", 0, 0, tiled=True)
    return mix(over_chan(turn(gated, 4)), w_out)


def solution(mesh):
    fine = Mesh(mesh.devices.reshape(8, 2, 4, 4, 2), ("z", "core", "x", "y_far", "y_near"))
    seq, chan = ("z", "core"), ("x", "y_far", "y_near")
    in_specs = (P(seq, chan), P(None, None, chan), P(chan, None), P(chan), P(None, chan))
    return jax.shard_map(shards, mesh=fine, in_specs=in_specs, out_specs=P(seq, chan), check_vma=False)
```

time: 137 us -> 127 us (0.927)
  the two profiles are of different devices: /device:TPU:1 before, /device:TPU:16 now
where the time goes in v2:
time: 127 us; the launch traced here: 126 us
  blocking collectives  121 us (95%)
  Pallas kernels  3.4 us (3%)
  local copies, waits for them, and re-layouts  1.84 us (1%)
    all_to_all x2, blocking collectives, over_chan(): whole = lax.all_to_all(copies(rows, 8), ('x', 'y_near'), 0, 0, tiled=True)  60 us
    all_to_all x2, blocking collectives, over_chan(): rows = lax.all_to_all(blocks, 'y_far', 0, 0, tiled=True)  29.1 us
    all_to_all x1, blocking collectives, shards(): pieces = lax.all_to_all(pieces, 'z', 0, 0, tiled=True)  19.2 us
    all_to_all x1, blocking collectives, shards(): gated = lax.all_to_all(gated, 'z', 0, 0, tiled=True)  10.7 us

profile of v2, /device:TPU:16, one launch (start us, length us, event | category | flops | bytes accessed | tf_op | source)
XLA Modules:
  0.0 126.3 jit_solution(16868733710418996853)
XLA Ops:
  0.0 0.9 broadcast_in_dim.6
  0.9 16.5 %all_to_all.30 = bf16[4,256,128]{2,1,0:T(8,128)(2,1)S(1)} all-to-all(bf16[4,256,128]{2,1,0:T(8,128)(2,1)S(1)} %broadcast_in_dim.6), channel_id=1, replica_groups=mesh['z'=8,'core'=2,'x'=4,'y_far'=4,'y_near'=2] {'y_far'}, dimensions={0} | all-to-all | bytes 524288 | tf_op jit(solution)/shard_map/all_to_all | solution.py:23
  17.4 0.5 broadcast_in_dim.7
  17.9 0.0 copy-start
  17.9 31.4 %all_to_all.31 = bf16[8,4,256,128]{3,2,1,0:T(8,128)(2,1)S(1)} all-to-all(bf16[8,4,256,128]{3,2,1,0:T(8,128)(2,1)S(1)} %broadcast_in_dim.7), channel_id=1, replica_groups=mesh['z'=8,'core'=2,'x'=4,'y_far'=4,'y_near'=2] {'x','y_near'}, dimensions={0} | all-to-all | bytes 4194304 | tf_op jit(solution)/shard_map/all_to_all | solution.py:24
  49.3 0.0 copy-done
  49.3 0.0 copy-start.2
  49.3 0.0 copy-start.3
  49.3 1.3 %project.1 = bf16[8,32,256]{2,1,0:T(8,128)(2,1)S(1)} custom-call(bf16[4,2,4,256,128]{4,3,2,1,0:T(8,128)(2,1)S(1)} %bitcast.6, bf16[3,4096,128]{2,1,0:T(8,128)(2,1)S(1)} %bitcast.7), custom_call_target="tpu_custom_call" | custom-call | tf_op jit(solution)/shard_map/project/pallas_call | solution.py:48
  50.6 19.2 %all_to_all.32 = bf16[8,32,256]{2,1,0:T(8,128)(2,1)S(1)} all-to-all(bf16[8,32,256]{2,1,0:T(8,128)(2,1)S(1)} %project.1), channel_id=1, replica_groups=mesh['z'=8,'core'=2,'x'=4,'y_far'=4,'y_near'=2] {'z'}, dimensions={0} | all-to-all | bytes 262144 | tf_op jit(solution)/shard_map/all_to_all | solution.py:165
  69.8 2.0 %all-gather = bf16[16,32,256]{2,1,0:T(8,128)(2,1)S(1)} all-gather(bf16[8,32,256]{2,1,0:T(8,128)(2,1)S(1)} %all_to_all.32), channel_id=2, replica_groups=mesh['z'=8,'core'=2,'x'=4,'y_far'=4,'y_near'=2] {'core'}, dimensions={0}, use_global_device_ids=true | all-gather | bytes 393216 | tf_op jit(solution)/shard_map/all_gather | solution.py:166
  71.8 0.0 copy-done.2
  71.8 0.0 copy-done.3
  71.8 0.7 convolve.1
  72.5 10.7 %all_to_all.33.g_ref = bf16[8,16,256]{2,1,0:T(8,128)(2,1)S(1)} all-to-all(bf16[8,16,256]{2,1,0:T(8,128)(2,1)S(1)} %convolve.1), channel_id=1, replica_groups=mesh['z'=8,'core'=2,'x'=4,'y_far'=4,'y_near'=2] {'z'}, dimensions={0} | all-to-all | bytes 131072 | tf_op jit(solution)/shard_map/all_to_all | solution.py:167
  83.2 0.1 turn.1
  83.3 12.6 %all_to_all.34 = bf16[4,256,128]{2,1,0:T(8,128)(2,1)S(1)} all-to-all(bf16[4,256,128]{2,1,0:T(8,128)(2,1)S(1)} %turn.1), channel_id=1, replica_groups=mesh['z'=8,'core'=2,'x'=4,'y_far'=4,'y_near'=2] {'y_far'}, dimensions={0} | all-to-all | bytes 524288 | tf_op jit(solution)/shard_map/all_to_all | solution.py:23
  95.9 0.5 broadcast_in_dim.8
  96.4 0.0 copy-start.1
  96.4 28.6 %all_to_all.35 = bf16[8,4,256,128]{3,2,1,0:T(8,128)(2,1)S(1)} all-to-all(bf16[8,4,256,128]{3,2,1,0:T(8,128)(2,1)S(1)} %broadcast_in_dim.8), channel_id=1, replica_groups=mesh['z'=8,'core'=2,'x'=4,'y_far'=4,'y_near'=2] {'x','y_near'}, dimensions={0} | all-to-all | bytes 4194304 | tf_op jit(solution)/shard_map/all_to_all | solution.py:24
  125.0 0.0 copy-done.1
  125.0 1.3 %mix.1 = bf16[256,128]{1,0:T(8,128)(2,1)} custom-call(bf16[4,2,4,256,128]{4,3,2,1,0:T(8,128)(2,1)S(1)} %bitcast.5, bf16[4096,128]{1,0:T(8,128)(2,1)S(1)} %copy-done.1), custom_call_target="tpu_custom_call" | custom-call | tf_op jit(solution)/shard_map/mix/pallas_call | solution.py:153
Async XLA Ops:
  17.9 31.4 %copy-start = (bf16[4096,3,128]{2,0,1:T(8,128)(2,1)S(1)}, bf16[4096,3,128]{2,0,1:T(8,128)(2,1)}, u32[]{:S(2)}) copy-start(bf16[4096,3,128]{2,0,1:T(8,128)(2,1)} %param.6) | copy-start | bytes 9437188
  49.3 22.5 %copy-start.2 = (bf16[8,4096]{1,0:T(8,128)(2,1)S(1)}, bf16[8,4096]{1,0:T(8,128)(2,1)}, u32[]{:S(2)}) copy-start(bf16[8,4096]{1,0:T(8,128)(2,1)} %filters_ref.1) | copy-start | bytes 196612
  49.3 22.5 %copy-start.3 = (f32[128]{0:T(128)S(1)}, f32[128]{0:T(128)}, u32[]{:S(2)}) copy-start(f32[128]{0:T(128)} %param.8) | copy-start | bytes 1540
  96.4 28.6 %copy-start.1 = (bf16[4096,128]{1,0:T(8,128)(2,1)S(1)}, bf16[4096,128]{1,0:T(8,128)(2,1)}, u32[]{:S(2)}) copy-start(bf16[4096,128]{1,0:T(8,128)(2,1)} %w_ref.1) | copy-start | bytes 3145732

commit v3 on v2

--- a/solution.py
+++ b/solution.py
@@ -15,23 +15,44 @@
     return pl.BlockSpec(*shape_and_map, memory_space=pltpu.VMEM)
 
 
-def copies(block, count):
-    return jnp.broadcast_to(block[None], (count,) + block.shape)
-
-
-def over_chan(blocks):
-    rows = lax.all_to_all(blocks, "y_far", 0, 0, tiled=True)
-    whole = lax.all_to_all(copies(rows, 8), ("x", "y_near"), 0, 0, tiled=True)
-    return whole.reshape((4, 2) + rows.shape)
-
-
-def project_kernel(x_ref, w_ref, out_ref):
-    steps, near, far, tokens, depth = x_ref.shape
-    chans = w_ref.shape[2]
-    span = near * far * depth
+def pack_kernel(x_ref, w_ref, out_ref):
+    core = lax.axis_index("core")
+    far, tokens, _ = x_ref.shape
+    depth = w_ref.shape[1]
+    half = far // 2
+    x = x_ref[...].reshape(far * tokens, -1)
+    for peer in range(out_ref.shape[0]):
+        out_ref[peer, : far * tokens] = x
+        for i in range(half):
+            slab = peer // 2 * 2 * far + (half * core + i) * 2 + peer % 2
+            at = far * tokens + i * depth
+            out_ref[peer, at : at + depth] = w_ref[slab]
+
+
+def pack(x, w, peers):
+    far, tokens, depth = x.shape
+    rows = w.shape[0] // (2 * peers)
+    return pl.pallas_call(
+        pack_kernel,
+        in_specs=[vmem(), vmem()],
+        out_specs=vmem(),
+        out_shape=jax.ShapeDtypeStruct((peers, far * tokens + rows, depth), x.dtype),
+        compiler_params=PARAMS,
+        name="pack",
+    )(x, w.reshape(-1, depth, w.shape[1]))
+
+
+def project_kernel(x_ref, w_ref, out_ref, rows_ref):
+    depth, chans = x_ref.shape[2], w_ref.shape[2]
+    tokens = out_ref.shape[2]
+    far = w_ref.shape[1] // (x_ref.shape[0] * depth)
+    span = 2 * far * depth
+    rows_ref[...] = x_ref[:, far * tokens :]
     acc = None
-    for step in range(steps):
-        left = jnp.concatenate([x_ref[step, j, i] for i in range(far) for j in range(near)], axis=1)
+    for step in range(x_ref.shape[0] // 2):
+        left = jnp.concatenate(
+            [x_ref[2 * step + j, i * tokens : (i + 1) * tokens] for i in range(far) for j in range(2)], axis=1
+        )
         right = jnp.concatenate([w_ref[i, step * span : (step + 1) * span] for i in range(3)], axis=1)
         part = jnp.dot(left, right, preferred_element_type=jnp.float32)
         acc = part if acc is None else acc + part
@@ -43,13 +64,17 @@
     out_ref[:, GROUP:, :] = query.T.astype(jnp.bfloat16).reshape(groups, GROUP, -1)
 
 
-def project(x, w):
-    tokens, chans = x.shape[3], w.shape[2]
+def project(x, w, tokens):
+    chans = w.shape[2]
+    rows = x.shape[1] - w.shape[1] // (x.shape[0] * x.shape[2]) * tokens
     return pl.pallas_call(
         project_kernel,
         in_specs=[vmem(), vmem()],
-        out_specs=vmem(),
-        out_shape=jax.ShapeDtypeStruct((chans // GROUP, 2 * GROUP, tokens), jnp.bfloat16),
+        out_specs=[vmem(), vmem()],
+        out_shape=[
+            jax.ShapeDtypeStruct((chans // GROUP, 2 * GROUP, tokens), jnp.bfloat16),
+            jax.ShapeDtypeStruct((x.shape[0], rows, x.shape[2]), jnp.bfloat16),
+        ],
         compiler_params=PARAMS,
         name="project",
     )(x, w)
@@ -98,17 +123,19 @@
     skip = jnp.concatenate([skip] * (block // LANES), axis=1)
     skip = jnp.concatenate([skip] * blocks, axis=0)
     gated = query.astype(jnp.float32) * (acc_ref[...] + skip * source.astype(jnp.float32))
-    out_ref[...] = gated.astype(jnp.bfloat16).reshape(out_ref.shape)
-
-
-def convolve(pieces, filters, skip):
+    gated = gated.astype(jnp.bfloat16).reshape(out_ref.shape[1:])
+    for i in range(out_ref.shape[0]):
+        out_ref[i] = gated
+
+
+def convolve(pieces, filters, skip, count):
     _, blocks, _, block = pieces.shape
     rows = blocks * GROUP
     return pl.pallas_call(
         conv_kernel,
         in_specs=[vmem(), vmem(), vmem()],
         out_specs=vmem(),
-        out_shape=jax.ShapeDtypeStruct((blocks, GROUP, block), jnp.bfloat16),
+        out_shape=jax.ShapeDtypeStruct((count, blocks, GROUP, block), jnp.bfloat16),
         scratch_shapes=[
             pltpu.VMEM((rows + GROUP, block), jnp.bfloat16),
             pltpu.VMEM((LANES, LANES + filters.shape[1]), jnp.bfloat16),
@@ -120,52 +147,67 @@
     )(pieces, filters, skip)
 
 
-def turn_kernel(g_ref, out_ref):
-    turned = g_ref[...].astype(jnp.float32).reshape(-1, g_ref.shape[2]).T.astype(jnp.bfloat16)
-    for i in range(out_ref.shape[0]):
-        out_ref[i] = turned
-
-
-def turn(gated, copies):
-    sources, rows, tokens = gated.shape
-    return pl.pallas_call(
-        turn_kernel,
+def mix_kernel(g_ref, own_ref, other_ref, out_ref, turned_ref):
+    core = lax.axis_index("core")
+    far, _, _, tokens = g_ref.shape
+    peers, rows, chans = own_ref.shape
+    for i in range(far):
+        turned_ref[i] = g_ref[i].astype(jnp.float32).reshape(-1, tokens).T.astype(jnp.bfloat16)
+    half = far // 2
+    acc = None
+    for w_ref, at in ((own_ref, core), (other_ref, 1 - core)):
+        left = jnp.concatenate([turned_ref[half * at + i] for i in range(half)], axis=1)
+        right = jnp.concatenate([w_ref[peer] for peer in range(peers)], axis=1)
+        part = jnp.dot(left, right, preferred_element_type=jnp.float32)
+        acc = part if acc is None else acc + part
+    for peer in range(peers):
+        out_ref[peer] = acc[:, peer * chans : (peer + 1) * chans].astype(jnp.bfloat16)
+
+
+def mix(gated, own, other):
+    far, groups, rows, tokens = gated.shape
+    peers, _, chans = own.shape
+    return pl.pallas_call(
+        mix_kernel,
+        in_specs=[vmem(), vmem(), vmem()],
+        out_specs=vmem(),
+        out_shape=jax.ShapeDtypeStruct((peers, tokens, chans), jnp.bfloat16),
+        scratch_shapes=[pltpu.VMEM((far, tokens, groups * rows), jnp.bfloat16)],
+        compiler_params=PARAMS,
+        name="mix",
+    )(gated, own, other)
+
+
+def add_kernel(parts_ref, out_ref):
+    total = parts_ref[0].astype(jnp.float32)
+    for i in range(1, parts_ref.shape[0]):
+        total += parts_ref[i].astype(jnp.float32)
+    out_ref[...] = total.astype(jnp.bfloat16)
+
+
+def add(parts):
+    return pl.pallas_call(
+        add_kernel,
         in_specs=[vmem()],
         out_specs=vmem(),
-        out_shape=jax.ShapeDtypeStruct((copies, tokens, sources * rows), jnp.bfloat16),
-        compiler_params=PARAMS,
-        name="turn",
-    )(gated)
-
-
-def mix_kernel(g_ref, w_ref, out_ref):
-    steps, near, far, tokens, depth = g_ref.shape
-    span = near * far * depth
-    acc = None
-    for step in range(steps):
-        left = jnp.concatenate([g_ref[step, j, i] for i in range(far) for j in range(near)], axis=1)
-        part = jnp.dot(left, w_ref[step * span : (step + 1) * span], preferred_element_type=jnp.float32)
-        acc = part if acc is None else acc + part
-    out_ref[...] = acc.astype(jnp.bfloat16)
-
-
-def mix(gated, w):
-    return pl.pallas_call(
-        mix_kernel,
-        in_specs=[vmem(), vmem()],
-        out_specs=vmem(),
-        out_shape=jax.ShapeDtypeStruct((gated.shape[3], w.shape[1]), jnp.bfloat16),
-        compiler_params=PARAMS,
-        name="mix",
-    )(gated, w)
+        out_shape=jax.ShapeDtypeStruct(parts.shape[1:], jnp.bfloat16),
+        compiler_params=PARAMS,
+        name="add",
+    )(parts)
 
 
 def shards(tokens, w_in, filters, skip, w_out):
-    pieces = project(over_chan(copies(tokens, 4)), w_in.transpose(1, 0, 2))
+    near = ("x", "y_near")
+    x = lax.all_gather(tokens, "y_far", axis=0)
+    x = lax.all_to_all(pack(x, w_out, 8), near, 0, 0, tiled=True)
+    pieces, own = project(x, w_in.transpose(1, 0, 2), tokens.shape[0])
+    other = lax.ppermute(own, "core", [(0, 1), (1, 0)])
     pieces = lax.all_to_all(pieces, "z", 0, 0, tiled=True)
-    gated = convolve(lax.all_gather(pieces, "core", axis=0), filters, skip.reshape(1, -1))
-    gated = lax.all_to_all(gated, "z", 0, 0, tiled=True)
-    return mix(over_chan(turn(gated, 4)), w_out)
+    gated = convolve(lax.all_gather(pieces, "core", axis=0), filters, skip.reshape(1, -1), 4)
+    shape = gated.shape
+    gated = lax.all_to_all(gated.reshape((-1,) + shape[2:]), ("y_far", "z"), 0, 0, tiled=True)
+    parts = mix(gated.reshape(shape), own, other)
+    return add(lax.all_to_all(parts, near, 0, 0, tiled=True))
 
 
 def solution(mesh):

time: 127 us -> 110 us (0.87)
  blocking collectives: 121 us -> 64 us
  waiting for transfers between devices: 0 us -> 21.4 us
  starting transfers between devices: 0 us -> 18 us
  Pallas kernels: 3.4 us -> 4.89 us
    all_to_all x6 -> x2, blocking collectives: 119 us -> 45.5 us  [the longest x1 33.9 us: shards(): x = lax.all_to_all(pack(x, w_out, 8), near, 0, 0, tiled=True)]
    all_to_all x0 -> x2, waiting for transfers between devices: none -> 21.4 us  [the longest x1 14.2 us: shards(): lax.all_to_all(gated.reshape((-1,) + shape[2:]), ('y_far', 'z'), 0, 0, ti...]
    all_gather x0 -> x1, blocking collectives: none -> 16.6 us  [shards(): x = lax.all_gather(tokens, 'y_far', axis=0)]
    all_to_all x0 -> x2, starting transfers between devices: none -> 16.1 us  [the longest x1 10.3 us: shards(): pieces = lax.all_to_all(pieces, 'z', 0, 0, tiled=True)]
    ppermute x0 -> x1, starting transfers between devices: none -> 1.91 us  [shards(): other = lax.ppermute(own, 'core', [(0, 1), (1, 0)])]
    broadcast_in_dim x3 -> x0, local copies, waits for them, and re-layouts: 1.82 us -> none  [copies(): return jnp.broadcast_to(block[None], (count,) + block.shape)]
    pallas_call x3 -> x4, Pallas kernels: 2.75 us -> 3.54 us  [the longest x1 2.01 us: project(): pl.pallas_call(project_kernel, in_specs=[vmem(), vmem()], out_specs=[vmem...]
  transfers between devices with their start and end apart: 0 -> 3, of which waited for: 0 -> 2; matrix products, arithmetic and copies ran while one was open for 0% -> 0% of each run, Pallas kernels for 0% -> 1%
where the time goes in v3:
time: 110 us
  blocking collectives  64 us (58%)
  waiting for transfers between devices  21.4 us (19%)
  starting transfers between devices  18 us (16%)
  Pallas kernels  4.89 us (4%)
  local copies, waits for them, and re-layouts  1.24 us (1%)
    all_to_all x1, blocking collectives, shards(): x = lax.all_to_all(pack(x, w_out, 8), near, 0, 0, tiled=True)  33.9 us
    all_gather x1, blocking collectives, shards(): x = lax.all_gather(tokens, 'y_far', axis=0)  16.6 us
    all_to_all x1, waiting for transfers between devices, shards(): lax.all_to_all(gated.reshape((-1,) + shape[2:]), ('y_far', 'z'), 0, 0, ti...  14.2 us
    all_to_all x1, blocking collectives, shards(): return add(lax.all_to_all(parts, near, 0, 0, tiled=True))  11.6 us
    all_to_all x1, starting transfers between devices, shards(): pieces = lax.all_to_all(pieces, 'z', 0, 0, tiled=True)  10.3 us
    all_to_all x1, waiting for transfers between devices, shards(): pieces = lax.all_to_all(pieces, 'z', 0, 0, tiled=True)  7.16 us
    all_to_all x1, starting transfers between devices, shards(): lax.all_to_all(gated.reshape((-1,) + shape[2:]), ('y_far', 'z'), 0, 0, ti...  5.84 us
  transfers between devices with their start and end apart: 3, of which 2 were waited for; matrix products, arithmetic and copies ran while one was open for 0% of the time, Pallas kernels for 1%

profile of v3, /device:TPU:16, one launch (start us, length us, event | category | flops | bytes accessed | tf_op | source)
XLA Modules:
  0.0 109.7 jit_solution(10000488137175841527)
XLA Ops:
  0.0 16.6 %all-gather = bf16[1024,128]{1,0:T(8,128)(2,1)S(1)} all-gather(bf16[256,128]{1,0:T(8,128)(2,1)} %param.5), channel_id=2, replica_groups=mesh['z'=8,'core'=2,'x'=4,'y_far'=4,'y_near'=2] {'y_far'}, dimensions={0}, use_global_device_ids=true | all-gather | bytes 327680 | tf_op jit(solution)/shard_map/all_gather | solution.py:201
  16.6 0.0 copy-start.1
  16.6 1.2 %copy-done.1 = bf16[4096,128]{1,0:T(8,128)(2,1)S(1)} copy-done((bf16[4096,128]{1,0:T(8,128)(2,1)S(1)}, bf16[4096,128]{1,0:T(8,128)(2,1)}, u32[]{:S(2)}) %copy-start.1) | copy-done | bytes 1048600
  17.8 0.3 pack.1
  18.1 0.0 copy-start
  18.1 33.9 %all_to_all.20.x_ref = bf16[8,1280,128]{2,1,0:T(8,128)(2,1)S(1)} all-to-all(bf16[8,1280,128]{2,1,0:T(8,128)(2,1)S(1)} %pack.1), channel_id=1, replica_groups=mesh['z'=8,'core'=2,'x'=4,'y_far'=4,'y_near'=2] {'x','y_near'}, dimensions={0} | all-to-all | bytes 5242880 | tf_op jit(solution)/shard_map/all_to_all | solution.py:202
  52.0 0.0 copy-done
  52.0 0.0 copy-start.2
  52.0 0.0 copy-start.3
  52.0 2.0 %project.1 = (bf16[8,32,256]{2,1,0:T(8,128)(2,1)}, bf16[8,256,128]{2,1,0:T(8,128)(2,1)S(1)}) custom-call(bf16[8,1280,128]{2,1,0:T(8,128)(2,1)S(1)} %all_to_all.20.x_ref, bf16[3,4096,128]{2,1,0:T(8,128)(2,1)S(1)} %bitcast.7), custom_call_target="tpu_custom_call" | custom-call | tf_op jit(solution)/shard_map/project/pallas_call | solution.py:70
  54.0 10.3 %all-to-all-start.1 = ((bf16[8,32,256]{2,1,0:T(8,128)(2,1)}), bf16[8,32,256]{2,1,0:T(8,128)(2,1)S(1)}, u32[]{:S(2)}, u32[]{:S(2)}) async-start(bf16[8,32,256]{2,1,0:T(8,128)(2,1)} %get-tuple-element.7), calls=%async_computation.1 | async-start | bytes 262144 | tf_op jit(solution)/shard_map/all_to_all | solution.py:205
  64.3 1.9 %collective-permute-start = (bf16[8,256,128]{2,1,0:T(8,128)(2,1)S(1)}, bf16[8,256,128]{2,1,0:T(8,128)(2,1)S(1)}, u32[]{:S(2)}, u32[]{:S(2)}) collective-permute-start(bf16[8,256,128]{2,1,0:T(8,128)(2,1)S(1)} %get-tuple-element.8.own_ref), channel_id=1, source_target_pairs={{0,32},{32,0},{1,33},{33,1},{2,34},{34,2},{3,35},{35,3},{4,36},{36... | collective-permute-start | bytes 1572872 | tf_op jit(solution)/shard_map/ppermute | solution.py:204
  66.2 7.2 %all-to-all-done.1 = bf16[8,32,256]{2,1,0:T(8,128)(2,1)S(1)} async-done(((bf16[8,32,256]{2,1,0:T(8,128)(2,1)}), bf16[8,32,256]{2,1,0:T(8,128)(2,1)S(1)}, u32[]{:S(2)}, u32[]{:S(2)}) %all-to-all-start.1) | async-done | bytes 131104 | tf_op jit(solution)/shard_map/all_to_all | solution.py:205
  73.4 2.0 %all-gather.1 = bf16[16,32,256]{2,1,0:T(8,128)(2,1)S(1)} all-gather(bf16[8,32,256]{2,1,0:T(8,128)(2,1)S(1)} %all-to-all-done.1), channel_id=3, replica_groups=mesh['z'=8,'core'=2,'x'=4,'y_far'=4,'y_near'=2] {'core'}, dimensions={0}, use_global_device_ids=true | all-gather | bytes 393216 | tf_op jit(solution)/shard_map/all_gather | solution.py:206
  75.4 0.0 copy-done.2
  75.4 0.0 copy-done.3
  75.4 1.4 %convolve.1 = bf16[4,8,16,256]{3,2,1,0:T(8,128)(2,1)} custom-call(bf16[2,8,32,256]{3,2,1,0:T(8,128)(2,1)S(1)} %bitcast.9, bf16[8,4096]{1,0:T(8,128)(2,1)S(1)} %copy-done.2, f32[1,128]{1,0:T(1,128)S(1)} %bitcast.12), custom_call_target="tpu_custom_call" | custom-call | tf_op jit(solution)/shard_map/convolve/pallas_call | solution.py:134
  76.7 5.8 %all-to-all-start.2 = ((bf16[32,16,256]{2,1,0:T(8,128)(2,1)}), bf16[32,16,256]{2,1,0:T(8,128)(2,1)S(1)}, u32[]{:S(2)}, u32[]{:S(2)}) async-start(bf16[32,16,256]{2,1,0:T(8,128)(2,1)} %bitcast.5), calls=%async_computation.2 | async-start | bytes 524288 | tf_op jit(solution)/shard_map/all_to_all | solution.py:208
  82.6 0.0 collective-permute-done.other_ref
  82.6 14.2 %all-to-all-done.2 = bf16[32,16,256]{2,1,0:T(8,128)(2,1)S(1)} async-done(((bf16[32,16,256]{2,1,0:T(8,128)(2,1)}), bf16[32,16,256]{2,1,0:T(8,128)(2,1)S(1)}, u32[]{:S(2)}, u32[]{:S(2)}) %all-to-all-start.2) | async-done | bytes 262176 | tf_op jit(solution)/shard_map/all_to_all | solution.py:208
  96.8 0.5 mix.1
  97.4 11.6 %all_to_all.21.parts_ref = bf16[8,256,128]{2,1,0:T(8,128)(2,1)S(1)} all-to-all(bf16[8,256,128]{2,1,0:T(8,128)(2,1)S(1)} %mix.1), channel_id=1, replica_groups=mesh['z'=8,'core'=2,'x'=4,'y_far'=4,'y_near'=2] {'x','y_near'}, dimensions={0} | all-to-all | bytes 1048576 | tf_op jit(solution)/shard_map/all_to_all | solution.py:210
  109.0 0.7 add.1
Async XLA Ops:
  16.6 1.2 %copy-start.1 = (bf16[4096,128]{1,0:T(8,128)(2,1)S(1)}, bf16[4096,128]{1,0:T(8,128)(2,1)}, u32[]{:S(2)}) copy-start(bf16[4096,128]{1,0:T(8,128)(2,1)} %param.9) | copy-start | bytes 3145732
  18.1 33.9 %copy-start = (bf16[4096,3,128]{2,0,1:T(8,128)(2,1)S(1)}, bf16[4096,3,128]{2,0,1:T(8,128)(2,1)}, u32[]{:S(2)}) copy-start(bf16[4096,3,128]{2,0,1:T(8,128)(2,1)} %param.6) | copy-start | bytes 9437188
  52.0 23.4 %copy-start.2 = (bf16[8,4096]{1,0:T(8,128)(2,1)S(1)}, bf16[8,4096]{1,0:T(8,128)(2,1)}, u32[]{:S(2)}) copy-start(bf16[8,4096]{1,0:T(8,128)(2,1)} %filters_ref.1) | copy-start | bytes 196612
  52.0 23.4 %copy-start.3 = (f32[128]{0:T(128)S(1)}, f32[128]{0:T(128)}, u32[]{:S(2)}) copy-start(f32[128]{0:T(128)} %param.8) | copy-start | bytes 1540
  54.0 19.4 %all-to-all-start.1 = ((bf16[8,32,256]{2,1,0:T(8,128)(2,1)}), bf16[8,32,256]{2,1,0:T(8,128)(2,1)S(1)}, u32[]{:S(2)}, u32[]{:S(2)}) async-start(bf16[8,32,256]{2,1,0:T(8,128)(2,1)} %get-tuple-element.7), calls=%async_computation.1 | async-start | bytes 262144 | tf_op jit(solution)/shard_map/all_to_all | solution.py:205
  64.3 18.3 %collective-permute-start = (bf16[8,256,128]{2,1,0:T(8,128)(2,1)S(1)}, bf16[8,256,128]{2,1,0:T(8,128)(2,1)S(1)}, u32[]{:S(2)}, u32[]{:S(2)}) collective-permute-start(bf16[8,256,128]{2,1,0:T(8,128)(2,1)S(1)} %get-tuple-element.8.own_ref), channel_id=1, source_target_pairs={{0,32},{32,0},{1,33},{33,1},{2,34},{34,2},{3,35},{35,3},{4,36},{36... | collective-permute-start | bytes 1572872 | tf_op jit(solution)/shard_map/ppermute | solution.py:204
  76.7 20.1 %all-to-all-start.2 = ((bf16[32,16,256]{2,1,0:T(8,128)(2,1)}), bf16[32,16,256]{2,1,0:T(8,128)(2,1)S(1)}, u32[]{:S(2)}, u32[]{:S(2)}) async-start(bf16[32,16,256]{2,1,0:T(8,128)(2,1)} %bitcast.5), calls=%async_computation.2 | async-start | bytes 524288 | tf_op jit(solution)/shard_map/all_to_all | solution.py:208

commit v4 on v3

--- a/solution.py
+++ b/solution.py
@@ -16,27 +16,22 @@
 
 
 def pack_kernel(x_ref, w_ref, out_ref):
-    core = lax.axis_index("core")
     far, tokens, _ = x_ref.shape
     depth = w_ref.shape[1]
-    half = far // 2
+    mine = 2 * lax.axis_index("core") + lax.rem(lax.axis_index("z"), 2)
     x = x_ref[...].reshape(far * tokens, -1)
     for peer in range(out_ref.shape[0]):
         out_ref[peer, : far * tokens] = x
-        for i in range(half):
-            slab = peer // 2 * 2 * far + (half * core + i) * 2 + peer % 2
-            at = far * tokens + i * depth
-            out_ref[peer, at : at + depth] = w_ref[slab]
+        out_ref[peer, far * tokens :] = w_ref[(peer // 2 * far + mine) * 2 + peer % 2]
 
 
 def pack(x, w, peers):
     far, tokens, depth = x.shape
-    rows = w.shape[0] // (2 * peers)
     return pl.pallas_call(
         pack_kernel,
         in_specs=[vmem(), vmem()],
         out_specs=vmem(),
-        out_shape=jax.ShapeDtypeStruct((peers, far * tokens + rows, depth), x.dtype),
+        out_shape=jax.ShapeDtypeStruct((peers, far * tokens + depth, depth), x.dtype),
         compiler_params=PARAMS,
         name="pack",
     )(x, w.reshape(-1, depth, w.shape[1]))
@@ -147,35 +142,37 @@
     )(pieces, filters, skip)
 
 
-def mix_kernel(g_ref, own_ref, other_ref, out_ref, turned_ref):
-    core = lax.axis_index("core")
+def mix_kernel(g_ref, *refs):
+    w_refs, out_ref, turned_ref = refs[:-2], refs[-2], refs[-1]
+    core, odd = lax.axis_index("core"), lax.rem(lax.axis_index("z"), 2)
     far, _, _, tokens = g_ref.shape
-    peers, rows, chans = own_ref.shape
+    peers, _, chans = w_refs[0].shape
     for i in range(far):
         turned_ref[i] = g_ref[i].astype(jnp.float32).reshape(-1, tokens).T.astype(jnp.bfloat16)
-    half = far // 2
     acc = None
-    for w_ref, at in ((own_ref, core), (other_ref, 1 - core)):
-        left = jnp.concatenate([turned_ref[half * at + i] for i in range(half)], axis=1)
-        right = jnp.concatenate([w_ref[peer] for peer in range(peers)], axis=1)
+    for pair, at in ((w_refs[:2], core), (w_refs[2:], 1 - core)):
+        left = jnp.concatenate([turned_ref[2 * at + odd], turned_ref[2 * at + 1 - odd]], axis=1)
+        right = jnp.concatenate(
+            [jnp.concatenate([w_ref[peer] for w_ref in pair], axis=0) for peer in range(peers)], axis=1
+        )
         part = jnp.dot(left, right, preferred_element_type=jnp.float32)
         acc = part if acc is None else acc + part
     for peer in range(peers):
         out_ref[peer] = acc[:, peer * chans : (peer + 1) * chans].astype(jnp.bfloat16)
 
 
-def mix(gated, own, other):
+def mix(gated, *w):
     far, groups, rows, tokens = gated.shape
-    peers, _, chans = own.shape
+    peers, _, chans = w[0].shape
     return pl.pallas_call(
         mix_kernel,
-        in_specs=[vmem(), vmem(), vmem()],
+        in_specs=[vmem()] * (1 + len(w)),
         out_specs=vmem(),
         out_shape=jax.ShapeDtypeStruct((peers, tokens, chans), jnp.bfloat16),
         scratch_shapes=[pltpu.VMEM((far, tokens, groups * rows), jnp.bfloat16)],
         compiler_params=PARAMS,
         name="mix",
-    )(gated, own, other)
+    )(gated, *w)
 
 
 def add_kernel(parts_ref, out_ref):
@@ -201,12 +198,13 @@
     x = lax.all_gather(tokens, "y_far", axis=0)
     x = lax.all_to_all(pack(x, w_out, 8), near, 0, 0, tiled=True)
     pieces, own = project(x, w_in.transpose(1, 0, 2), tokens.shape[0])
-    other = lax.ppermute(own, "core", [(0, 1), (1, 0)])
+    beside = lax.ppermute(own, "z", [(i, i ^ 1) for i in range(8)])
     pieces = lax.all_to_all(pieces, "z", 0, 0, tiled=True)
     gated = convolve(lax.all_gather(pieces, "core", axis=0), filters, skip.reshape(1, -1), 4)
+    others = [lax.ppermute(rows, "core", [(0, 1), (1, 0)]) for rows in (own, beside)]
     shape = gated.shape
     gated = lax.all_to_all(gated.reshape((-1,) + shape[2:]), ("y_far", "z"), 0, 0, tiled=True)
-    parts = mix(gated.reshape(shape), own, other)
+    parts = mix(gated.reshape(shape), own, beside, *others)
     return add(lax.all_to_all(parts, near, 0, 0, tiled=True))
 
 

time: 110 us -> 107 us (0.973)
  the two profiles are of different devices: /device:TPU:16 before, /device:TPU:1 now
where the time goes in v4:
time: 107 us; the launch traced here: 106 us
  blocking collectives  64 us (60%)
  starting transfers between devices  23.5 us (22%)
  waiting for transfers between devices  12.5 us (12%)
  Pallas kernels  4.87 us (5%)
  local copies, waits for them, and re-layouts  1.24 us (1%)
    all_to_all x1, blocking collectives, shards(): x = lax.all_to_all(pack(x, w_out, 8), near, 0, 0, tiled=True)  28.7 us
    all_gather x1, blocking collectives, shards(): x = lax.all_gather(tokens, 'y_far', axis=0)  15.7 us
    all_to_all x1, blocking collectives, shards(): return add(lax.all_to_all(parts, near, 0, 0, tiled=True))  12 us
    all_to_all x1, starting transfers between devices, shards(): pieces = lax.all_to_all(pieces, 'z', 0, 0, tiled=True)  11.2 us
    all_gather x1, blocking collectives, shards(): lax.all_gather(pieces, 'core', axis=0)  7.61 us
    all_to_all x1, waiting for transfers between devices, shards(): lax.all_to_all(gated.reshape((-1,) + shape[2:]), ('y_far', 'z'), 0, 0, ti...  6.33 us
    all_to_all x1, waiting for transfers between devices, shards(): pieces = lax.all_to_all(pieces, 'z', 0, 0, tiled=True)  4.67 us
    ppermute x2, starting transfers between devices, shards(): lax.ppermute(rows, 'core', [(0, 1), (1, 0)])  4.47 us
  transfers between devices with their start and end apart: 5, of which 3 were waited for; matrix products, arithmetic and copies ran while one was open for 0% of the time, Pallas kernels for 1%

profile of v4, /device:TPU:1, one launch (start us, length us, event | category | flops | bytes accessed | tf_op | source)
XLA Modules:
  0.0 106.2 jit_solution(4389572533826732917)
XLA Ops:
  0.0 15.7 %all-gather = bf16[1024,128]{1,0:T(8,128)(2,1)S(1)} all-gather(bf16[256,128]{1,0:T(8,128)(2,1)} %param.5), channel_id=2, replica_groups=mesh['z'=8,'core'=2,'x'=4,'y_far'=4,'y_near'=2] {'y_far'}, dimensions={0}, use_global_device_ids=true | all-gather | bytes 327680 | tf_op jit(solution)/shard_map/all_gather | solution.py:198
  15.7 0.0 copy-start.1
  15.7 1.2 %copy-done.1 = bf16[4096,128]{1,0:T(8,128)(2,1)S(1)} copy-done((bf16[4096,128]{1,0:T(8,128)(2,1)S(1)}, bf16[4096,128]{1,0:T(8,128)(2,1)}, u32[]{:S(2)}) %copy-start.1) | copy-done | bytes 1048600
  16.9 0.3 pack.1
  17.2 0.0 copy-start
  17.2 28.7 %all_to_all.20.x_ref = bf16[8,1152,128]{2,1,0:T(8,128)(2,1)S(1)} all-to-all(bf16[8,1152,128]{2,1,0:T(8,128)(2,1)S(1)} %pack.1), channel_id=1, replica_groups=mesh['z'=8,'core'=2,'x'=4,'y_far'=4,'y_near'=2] {'x','y_near'}, dimensions={0} | all-to-all | bytes 4718592 | tf_op jit(solution)/shard_map/all_to_all | solution.py:199
  45.9 0.0 copy-done
  45.9 0.0 copy-start.2
  45.9 0.0 copy-start.3
  45.9 2.0 %project.1 = (bf16[8,32,256]{2,1,0:T(8,128)(2,1)}, bf16[8,128,128]{2,1,0:T(8,128)(2,1)S(1)}) custom-call(bf16[8,1152,128]{2,1,0:T(8,128)(2,1)S(1)} %all_to_all.20.x_ref, bf16[3,4096,128]{2,1,0:T(8,128)(2,1)S(1)} %bitcast.7), custom_call_target="tpu_custom_call" | custom-call | tf_op jit(solution)/shard_map/project/pallas_call | solution.py:65
  47.9 11.2 %all-to-all-start.1 = ((bf16[8,32,256]{2,1,0:T(8,128)(2,1)}), bf16[8,32,256]{2,1,0:T(8,128)(2,1)S(1)}, u32[]{:S(2)}, u32[]{:S(2)}) async-start(bf16[8,32,256]{2,1,0:T(8,128)(2,1)} %get-tuple-element.7), calls=%async_computation.1 | async-start | bytes 262144 | tf_op jit(solution)/shard_map/all_to_all | solution.py:202
  59.1 3.4 %collective-permute-start = (bf16[8,128,128]{2,1,0:T(8,128)(2,1)S(1)}, bf16[8,128,128]{2,1,0:T(8,128)(2,1)S(1)}, u32[]{:S(2)}, u32[]{:S(2)}) collective-permute-start(bf16[8,128,128]{2,1,0:T(8,128)(2,1)S(1)} %get-tuple-element.8.refs_0_), channel_id=1, source_target_pairs={{0,64},{64,0},{128,192},{192,128},{256,320},{320,256},{384,448},{4... | collective-permute-start | bytes 786440 | tf_op jit(solution)/shard_map/ppermute | solution.py:201
  62.5 4.7 %all-to-all-done.1 = bf16[8,32,256]{2,1,0:T(8,128)(2,1)S(1)} async-done(((bf16[8,32,256]{2,1,0:T(8,128)(2,1)}), bf16[8,32,256]{2,1,0:T(8,128)(2,1)S(1)}, u32[]{:S(2)}, u32[]{:S(2)}) %all-to-all-start.1) | async-done | bytes 131104 | tf_op jit(solution)/shard_map/all_to_all | solution.py:202
  67.1 7.6 %all-gather.1 = bf16[16,32,256]{2,1,0:T(8,128)(2,1)S(1)} all-gather(bf16[8,32,256]{2,1,0:T(8,128)(2,1)S(1)} %all-to-all-done.1), channel_id=3, replica_groups=mesh['z'=8,'core'=2,'x'=4,'y_far'=4,'y_near'=2] {'core'}, dimensions={0}, use_global_device_ids=true | all-gather | bytes 393216 | tf_op jit(solution)/shard_map/all_gather | solution.py:203
  74.7 0.0 copy-done.2
  74.7 0.0 copy-done.3
  74.8 1.4 %convolve.1 = bf16[4,8,16,256]{3,2,1,0:T(8,128)(2,1)} custom-call(bf16[2,8,32,256]{3,2,1,0:T(8,128)(2,1)S(1)} %bitcast.11, bf16[8,4096]{1,0:T(8,128)(2,1)S(1)} %copy-done.2, f32[1,128]{1,0:T(1,128)S(1)} %bitcast.12), custom_call_target="tpu_custom_call" | custom-call | tf_op jit(solution)/shard_map/convolve/pallas_call | solution.py:129
  76.1 4.4 %all-to-all-start.2 = ((bf16[32,16,256]{2,1,0:T(8,128)(2,1)}), bf16[32,16,256]{2,1,0:T(8,128)(2,1)S(1)}, u32[]{:S(2)}, u32[]{:S(2)}) async-start(bf16[32,16,256]{2,1,0:T(8,128)(2,1)} %bitcast.5), calls=%async_computation.2 | async-start | bytes 524288 | tf_op jit(solution)/shard_map/all_to_all | solution.py:206
  80.6 2.5 %collective-permute-start.1 = (bf16[8,128,128]{2,1,0:T(8,128)(2,1)S(1)}, bf16[8,128,128]{2,1,0:T(8,128)(2,1)S(1)}, u32[]{:S(2)}, u32[]{:S(2)}) collective-permute-start(bf16[8,128,128]{2,1,0:T(8,128)(2,1)S(1)} %get-tuple-element.8.refs_0_), channel_id=1, source_target_pairs={{0,32},{32,0},{1,33},{33,1},{2,34},{34,2},{3,35},{35,3},{4,36},{36... | collective-permute-start | bytes 786440 | tf_op jit(solution)/shard_map/ppermute | solution.py:204
  83.1 0.0 collective-permute-done.refs_1_
  83.1 1.9 %collective-permute-start.2 = (bf16[8,128,128]{2,1,0:T(8,128)(2,1)S(1)}, bf16[8,128,128]{2,1,0:T(8,128)(2,1)S(1)}, u32[]{:S(2)}, u32[]{:S(2)}) collective-permute-start(bf16[8,128,128]{2,1,0:T(8,128)(2,1)S(1)} %collective-permute-done.refs_1_), channel_id=1, source_target_pairs={{0,32},{32,0},{1,33},{33,1},{2,34},{34,2},{3,35},{35,3},{4,36},{36... | collective-permute-start | bytes 786440 | tf_op jit(solution)/shard_map/ppermute | solution.py:204
  85.0 0.0 collective-permute-done.1.refs_2_
  85.1 1.5 %collective-permute-done.2.refs_3_ = bf16[8,128,128]{2,1,0:T(8,128)(2,1)S(1)} collective-permute-done((bf16[8,128,128]{2,1,0:T(8,128)(2,1)S(1)}, bf16[8,128,128]{2,1,0:T(8,128)(2,1)S(1)}, u32[]{:S(2)}, u32[]{:S(2)}) %collective-permute-start.2) | collective-permute-done | bytes 262176 | tf_op jit(solution)/shard_map/ppermute | solution.py:204
  86.6 6.3 %all-to-all-done.2 = bf16[32,16,256]{2,1,0:T(8,128)(2,1)S(1)} async-done(((bf16[32,16,256]{2,1,0:T(8,128)(2,1)}), bf16[32,16,256]{2,1,0:T(8,128)(2,1)S(1)}, u32[]{:S(2)}, u32[]{:S(2)}) %all-to-all-start.2) | async-done | bytes 262176 | tf_op jit(solution)/shard_map/all_to_all | solution.py:206
  92.9 0.5 mix.1
  93.4 12.0 %all_to_all.21.parts_ref = bf16[8,256,128]{2,1,0:T(8,128)(2,1)S(1)} all-to-all(bf16[8,256,128]{2,1,0:T(8,128)(2,1)S(1)} %mix.1), channel_id=1, replica_groups=mesh['z'=8,'core'=2,'x'=4,'y_far'=4,'y_near'=2] {'x','y_near'}, dimensions={0} | all-to-all | bytes 1048576 | tf_op jit(solution)/shard_map/all_to_all | solution.py:208
  105.5 0.7 add.1
Async XLA Ops:
  15.7 1.2 %copy-start.1 = (bf16[4096,128]{1,0:T(8,128)(2,1)S(1)}, bf16[4096,128]{1,0:T(8,128)(2,1)}, u32[]{:S(2)}) copy-start(bf16[4096,128]{1,0:T(8,128)(2,1)} %param.9) | copy-start | bytes 3145732
  17.2 28.7 %copy-start = (bf16[4096,3,128]{2,0,1:T(8,128)(2,1)S(1)}, bf16[4096,3,128]{2,0,1:T(8,128)(2,1)}, u32[]{:S(2)}) copy-start(bf16[4096,3,128]{2,0,1:T(8,128)(2,1)} %param.6) | copy-start | bytes 9437188
  45.9 28.9 %copy-start.2 = (bf16[8,4096]{1,0:T(8,128)(2,1)S(1)}, bf16[8,4096]{1,0:T(8,128)(2,1)}, u32[]{:S(2)}) copy-start(bf16[8,4096]{1,0:T(8,128)(2,1)} %filters_ref.1) | copy-start | bytes 196612
  45.9 28.9 %copy-start.3 = (f32[128]{0:T(128)S(1)}, f32[128]{0:T(128)}, u32[]{:S(2)}) copy-start(f32[128]{0:T(128)} %param.8) | copy-start | bytes 1540
  47.9 19.3 %all-to-all-start.1 = ((bf16[8,32,256]{2,1,0:T(8,128)(2,1)}), bf16[8,32,256]{2,1,0:T(8,128)(2,1)S(1)}, u32[]{:S(2)}, u32[]{:S(2)}) async-start(bf16[8,32,256]{2,1,0:T(8,128)(2,1)} %get-tuple-element.7), calls=%async_computation.1 | async-start | bytes 262144 | tf_op jit(solution)/shard_map/all_to_all | solution.py:202
  59.1 24.0 %collective-permute-start = (bf16[8,128,128]{2,1,0:T(8,128)(2,1)S(1)}, bf16[8,128,128]{2,1,0:T(8,128)(2,1)S(1)}, u32[]{:S(2)}, u32[]{:S(2)}) collective-permute-start(bf16[8,128,128]{2,1,0:T(8,128)(2,1)S(1)} %get-tuple-element.8.refs_0_), channel_id=1, source_target_pairs={{0,64},{64,0},{128,192},{192,128},{256,320},{320,256},{384,448},{4... | collective-permute-start | bytes 786440 | tf_op jit(solution)/shard_map/ppermute | solution.py:201
  76.1 16.8 %all-to-all-start.2 = ((bf16[32,16,256]{2,1,0:T(8,128)(2,1)}), bf16[32,16,256]{2,1,0:T(8,128)(2,1)S(1)}, u32[]{:S(2)}, u32[]{:S(2)}) async-start(bf16[32,16,256]{2,1,0:T(8,128)(2,1)} %bitcast.5), calls=%async_computation.2 | async-start | bytes 524288 | tf_op jit(solution)/shard_map/all_to_all | solution.py:206
  80.6 4.5 %collective-permute-start.1 = (bf16[8,128,128]{2,1,0:T(8,128)(2,1)S(1)}, bf16[8,128,128]{2,1,0:T(8,128)(2,1)S(1)}, u32[]{:S(2)}, u32[]{:S(2)}) collective-permute-start(bf16[8,128,128]{2,1,0:T(8,128)(2,1)S(1)} %get-tuple-element.8.refs_0_), channel_id=1, source_target_pairs={{0,32},{32,0},{1,33},{33,1},{2,34},{34,2},{3,35},{35,3},{4,36},{36... | collective-permute-start | bytes 786440 | tf_op jit(solution)/shard_map/ppermute | solution.py:204
  83.1 3.4 %collective-permute-start.2 = (bf16[8,128,128]{2,1,0:T(8,128)(2,1)S(1)}, bf16[8,128,128]{2,1,0:T(8,128)(2,1)S(1)}, u32[]{:S(2)}, u32[]{:S(2)}) collective-permute-start(bf16[8,128,128]{2,1,0:T(8,128)(2,1)S(1)} %collective-permute-done.refs_1_), channel_id=1, source_target_pairs={{0,32},{32,0},{1,33},{33,1},{2,34},{34,2},{3,35},{35,3},{4,36},{36... | collective-permute-start | bytes 786440 | tf_op jit(solution)/shard_map/ppermute | solution.py:204

commit v5 on v4

--- a/solution.py
+++ b/solution.py
@@ -15,26 +15,39 @@
     return pl.BlockSpec(*shape_and_map, memory_space=pltpu.VMEM)
 
 
-def pack_kernel(x_ref, w_ref, out_ref):
+def pack_kernel(x_ref, w_hbm, out_ref, sems):
     far, tokens, _ = x_ref.shape
-    depth = w_ref.shape[1]
+    depth = w_hbm.shape[1]
     mine = 2 * lax.axis_index("core") + lax.rem(lax.axis_index("z"), 2)
+    sends = [
+        pltpu.make_async_copy(
+            w_hbm.at[(peer // 2 * far + mine) * 2 + peer % 2],
+            out_ref.at[peer, pl.ds(far * tokens, depth)],
+            sems.at[peer],
+        )
+        for peer in range(out_ref.shape[0])
+    ]
+    for send in sends:
+        send.start()
     x = x_ref[...].reshape(far * tokens, -1)
     for peer in range(out_ref.shape[0]):
         out_ref[peer, : far * tokens] = x
-        out_ref[peer, far * tokens :] = w_ref[(peer // 2 * far + mine) * 2 + peer % 2]
+    for send in sends:
+        send.wait()
 
 
 def pack(x, w, peers):
     far, tokens, depth = x.shape
+    w = pltpu.with_memory_space_constraint(w.reshape(-1, depth, w.shape[1]), pltpu.HBM)
     return pl.pallas_call(
         pack_kernel,
-        in_specs=[vmem(), vmem()],
+        in_specs=[vmem(), pl.BlockSpec(memory_space=pltpu.HBM)],
         out_specs=vmem(),
         out_shape=jax.ShapeDtypeStruct((peers, far * tokens + depth, depth), x.dtype),
+        scratch_shapes=[pltpu.SemaphoreType.DMA((peers,))],
         compiler_params=PARAMS,
         name="pack",
-    )(x, w.reshape(-1, depth, w.shape[1]))
+    )(x, w)
 
 
 def project_kernel(x_ref, w_ref, out_ref, rows_ref):

time: 107 us -> 107 us (level)
  local copies, waits for them, and re-layouts: 1.24 us -> 0.01 us
    unnamed x8 -> x6, local copies, waits for them, and re-layouts: 1.24 us -> 0.01 us
where the time goes in v5:
time: 107 us; the launch traced here: 106 us
  blocking collectives  64 us (60%)
  starting transfers between devices  23.5 us (22%)
  waiting for transfers between devices  12.5 us (12%)
  Pallas kernels  5.56 us (5%)
    all_to_all x1, blocking collectives, shards(): x = lax.all_to_all(pack(x, w_out, 8), near, 0, 0, tiled=True)  28.7 us
    all_gather x1, blocking collectives, shards(): x = lax.all_gather(tokens, 'y_far', axis=0)  15.7 us
    all_to_all x1, blocking collectives, shards(): return add(lax.all_to_all(parts, near, 0, 0, tiled=True))  12.1 us
    all_to_all x1, starting transfers between devices, shards(): pieces = lax.all_to_all(pieces, 'z', 0, 0, tiled=True)  11.2 us
    all_gather x1, blocking collectives, shards(): lax.all_gather(pieces, 'core', axis=0)  7.61 us
    all_to_all x1, waiting for transfers between devices, shards(): lax.all_to_all(gated.reshape((-1,) + shape[2:]), ('y_far', 'z'), 0, 0, ti...  6.33 us
    all_to_all x1, waiting for transfers between devices, shards(): pieces = lax.all_to_all(pieces, 'z', 0, 0, tiled=True)  4.67 us
    ppermute x2, starting transfers between devices, shards(): lax.ppermute(rows, 'core', [(0, 1), (1, 0)])  4.46 us
  transfers between devices with their start and end apart: 5, of which 3 were waited for; matrix products, arithmetic and copies ran while one was open for 0% of the time, Pallas kernels for 1%

profile of v5, /device:TPU:1, one launch (start us, length us, event | category | flops | bytes accessed | tf_op | source)
XLA Modules:
  0.0 105.6 jit_solution(13180184143875220112)
XLA Ops:
  0.0 15.7 %all-gather = bf16[1024,128]{1,0:T(8,128)(2,1)S(1)} all-gather(bf16[256,128]{1,0:T(8,128)(2,1)} %param.5), channel_id=2, replica_groups=mesh['z'=8,'core'=2,'x'=4,'y_far'=4,'y_near'=2] {'y_far'}, dimensions={0}, use_global_device_ids=true | all-gather | bytes 327680 | tf_op jit(solution)/shard_map/all_gather | solution.py:211
  15.7 1.0 pack.1
  16.6 0.0 copy-start
  16.7 28.7 %all_to_all.20.x_ref = bf16[8,1152,128]{2,1,0:T(8,128)(2,1)S(1)} all-to-all(bf16[8,1152,128]{2,1,0:T(8,128)(2,1)S(1)} %pack.1), channel_id=1, replica_groups=mesh['z'=8,'core'=2,'x'=4,'y_far'=4,'y_near'=2] {'x','y_near'}, dimensions={0} | all-to-all | bytes 4718592 | tf_op jit(solution)/shard_map/all_to_all | solution.py:212
  45.3 0.0 copy-done
  45.3 0.0 copy-start.1
  45.3 0.0 copy-start.2
  45.3 2.0 %project.1 = (bf16[8,32,256]{2,1,0:T(8,128)(2,1)}, bf16[8,128,128]{2,1,0:T(8,128)(2,1)S(1)}) custom-call(bf16[8,1152,128]{2,1,0:T(8,128)(2,1)S(1)} %all_to_all.20.x_ref, bf16[3,4096,128]{2,1,0:T(8,128)(2,1)S(1)} %bitcast.7), custom_call_target="tpu_custom_call" | custom-call | tf_op jit(solution)/shard_map/project/pallas_call | solution.py:78
  47.3 11.2 %all-to-all-start.1 = ((bf16[8,32,256]{2,1,0:T(8,128)(2,1)}), bf16[8,32,256]{2,1,0:T(8,128)(2,1)S(1)}, u32[]{:S(2)}, u32[]{:S(2)}) async-start(bf16[8,32,256]{2,1,0:T(8,128)(2,1)} %get-tuple-element.7), calls=%async_computation.1 | async-start | bytes 262144 | tf_op jit(solution)/shard_map/all_to_all | solution.py:215
  58.5 3.4 %collective-permute-start = (bf16[8,128,128]{2,1,0:T(8,128)(2,1)S(1)}, bf16[8,128,128]{2,1,0:T(8,128)(2,1)S(1)}, u32[]{:S(2)}, u32[]{:S(2)}) collective-permute-start(bf16[8,128,128]{2,1,0:T(8,128)(2,1)S(1)} %get-tuple-element.8.refs_0_), channel_id=1, source_target_pairs={{0,64},{64,0},{128,192},{192,128},{256,320},{320,256},{384,448},{4... | collective-permute-start | bytes 786440 | tf_op jit(solution)/shard_map/ppermute | solution.py:214
  61.9 4.7 %all-to-all-done.1 = bf16[8,32,256]{2,1,0:T(8,128)(2,1)S(1)} async-done(((bf16[8,32,256]{2,1,0:T(8,128)(2,1)}), bf16[8,32,256]{2,1,0:T(8,128)(2,1)S(1)}, u32[]{:S(2)}, u32[]{:S(2)}) %all-to-all-start.1) | async-done | bytes 131104 | tf_op jit(solution)/shard_map/all_to_all | solution.py:215
  66.6 7.6 %all-gather.1 = bf16[16,32,256]{2,1,0:T(8,128)(2,1)S(1)} all-gather(bf16[8,32,256]{2,1,0:T(8,128)(2,1)S(1)} %all-to-all-done.1), channel_id=3, replica_groups=mesh['z'=8,'core'=2,'x'=4,'y_far'=4,'y_near'=2] {'core'}, dimensions={0}, use_global_device_ids=true | all-gather | bytes 393216 | tf_op jit(solution)/shard_map/all_gather | solution.py:216
  74.2 0.0 copy-done.1
  74.2 0.0 copy-done.2
  74.2 1.4 %convolve.1 = bf16[4,8,16,256]{3,2,1,0:T(8,128)(2,1)} custom-call(bf16[2,8,32,256]{3,2,1,0:T(8,128)(2,1)S(1)} %bitcast.10, bf16[8,4096]{1,0:T(8,128)(2,1)S(1)} %copy-done.1, f32[1,128]{1,0:T(1,128)S(1)} %bitcast.11), custom_call_target="tpu_custom_call" | custom-call | tf_op jit(solution)/shard_map/convolve/pallas_call | solution.py:142
  75.6 4.4 %all-to-all-start.2 = ((bf16[32,16,256]{2,1,0:T(8,128)(2,1)}), bf16[32,16,256]{2,1,0:T(8,128)(2,1)S(1)}, u32[]{:S(2)}, u32[]{:S(2)}) async-start(bf16[32,16,256]{2,1,0:T(8,128)(2,1)} %bitcast.5), calls=%async_computation.2 | async-start | bytes 524288 | tf_op jit(solution)/shard_map/all_to_all | solution.py:219
  80.0 2.5 %collective-permute-start.1 = (bf16[8,128,128]{2,1,0:T(8,128)(2,1)S(1)}, bf16[8,128,128]{2,1,0:T(8,128)(2,1)S(1)}, u32[]{:S(2)}, u32[]{:S(2)}) collective-permute-start(bf16[8,128,128]{2,1,0:T(8,128)(2,1)S(1)} %get-tuple-element.8.refs_0_), channel_id=1, source_target_pairs={{0,32},{32,0},{1,33},{33,1},{2,34},{34,2},{3,35},{35,3},{4,36},{36... | collective-permute-start | bytes 786440 | tf_op jit(solution)/shard_map/ppermute | solution.py:217
  82.6 0.0 collective-permute-done.refs_1_
  82.6 1.9 %collective-permute-start.2 = (bf16[8,128,128]{2,1,0:T(8,128)(2,1)S(1)}, bf16[8,128,128]{2,1,0:T(8,128)(2,1)S(1)}, u32[]{:S(2)}, u32[]{:S(2)}) collective-permute-start(bf16[8,128,128]{2,1,0:T(8,128)(2,1)S(1)} %collective-permute-done.refs_1_), channel_id=1, source_target_pairs={{0,32},{32,0},{1,33},{33,1},{2,34},{34,2},{3,35},{35,3},{4,36},{36... | collective-permute-start | bytes 786440 | tf_op jit(solution)/shard_map/ppermute | solution.py:217
  84.5 0.0 collective-permute-done.1.refs_2_
  84.5 1.5 %collective-permute-done.2.refs_3_ = bf16[8,128,128]{2,1,0:T(8,128)(2,1)S(1)} collective-permute-done((bf16[8,128,128]{2,1,0:T(8,128)(2,1)S(1)}, bf16[8,128,128]{2,1,0:T(8,128)(2,1)S(1)}, u32[]{:S(2)}, u32[]{:S(2)}) %collective-permute-start.2) | collective-permute-done | bytes 262176 | tf_op jit(solution)/shard_map/ppermute | solution.py:217
  86.0 6.3 %all-to-all-done.2 = bf16[32,16,256]{2,1,0:T(8,128)(2,1)S(1)} async-done(((bf16[32,16,256]{2,1,0:T(8,128)(2,1)}), bf16[32,16,256]{2,1,0:T(8,128)(2,1)S(1)}, u32[]{:S(2)}, u32[]{:S(2)}) %all-to-all-start.2) | async-done | bytes 262176 | tf_op jit(solution)/shard_map/all_to_all | solution.py:219
  92.3 0.5 mix.1
  92.9 12.1 %all_to_all.21.parts_ref = bf16[8,256,128]{2,1,0:T(8,128)(2,1)S(1)} all-to-all(bf16[8,256,128]{2,1,0:T(8,128)(2,1)S(1)} %mix.1), channel_id=1, replica_groups=mesh['z'=8,'core'=2,'x'=4,'y_far'=4,'y_near'=2] {'x','y_near'}, dimensions={0} | all-to-all | bytes 1048576 | tf_op jit(solution)/shard_map/all_to_all | solution.py:221
  104.9 0.7 add.1
Async XLA Ops:
  16.6 28.7 %copy-start = (bf16[4096,3,128]{2,0,1:T(8,128)(2,1)S(1)}, bf16[4096,3,128]{2,0,1:T(8,128)(2,1)}, u32[]{:S(2)}) copy-start(bf16[4096,3,128]{2,0,1:T(8,128)(2,1)} %param.6) | copy-start | bytes 9437188
  45.3 28.9 %copy-start.1 = (bf16[8,4096]{1,0:T(8,128)(2,1)S(1)}, bf16[8,4096]{1,0:T(8,128)(2,1)}, u32[]{:S(2)}) copy-start(bf16[8,4096]{1,0:T(8,128)(2,1)} %filters_ref.1) | copy-start | bytes 196612
  45.3 28.9 %copy-start.2 = (f32[128]{0:T(128)S(1)}, f32[128]{0:T(128)}, u32[]{:S(2)}) copy-start(f32[128]{0:T(128)} %param.8) | copy-start | bytes 1540
  47.3 19.3 %all-to-all-start.1 = ((bf16[8,32,256]{2,1,0:T(8,128)(2,1)}), bf16[8,32,256]{2,1,0:T(8,128)(2,1)S(1)}, u32[]{:S(2)}, u32[]{:S(2)}) async-start(bf16[8,32,256]{2,1,0:T(8,128)(2,1)} %get-tuple-element.7), calls=%async_computation.1 | async-start | bytes 262144 | tf_op jit(solution)/shard_map/all_to_all | solution.py:215
  58.5 24.0 %collective-permute-start = (bf16[8,128,128]{2,1,0:T(8,128)(2,1)S(1)}, bf16[8,128,128]{2,1,0:T(8,128)(2,1)S(1)}, u32[]{:S(2)}, u32[]{:S(2)}) collective-permute-start(bf16[8,128,128]{2,1,0:T(8,128)(2,1)S(1)} %get-tuple-element.8.refs_0_), channel_id=1, source_target_pairs={{0,64},{64,0},{128,192},{192,128},{256,320},{320,256},{384,448},{4... | collective-permute-start | bytes 786440 | tf_op jit(solution)/shard_map/ppermute | solution.py:214
  75.6 16.8 %all-to-all-start.2 = ((bf16[32,16,256]{2,1,0:T(8,128)(2,1)}), bf16[32,16,256]{2,1,0:T(8,128)(2,1)S(1)}, u32[]{:S(2)}, u32[]{:S(2)}) async-start(bf16[32,16,256]{2,1,0:T(8,128)(2,1)} %bitcast.5), calls=%async_computation.2 | async-start | bytes 524288 | tf_op jit(solution)/shard_map/all_to_all | solution.py:219
  80.0 4.5 %collective-permute-start.1 = (bf16[8,128,128]{2,1,0:T(8,128)(2,1)S(1)}, bf16[8,128,128]{2,1,0:T(8,128)(2,1)S(1)}, u32[]{:S(2)}, u32[]{:S(2)}) collective-permute-start(bf16[8,128,128]{2,1,0:T(8,128)(2,1)S(1)} %get-tuple-element.8.refs_0_), channel_id=1, source_target_pairs={{0,32},{32,0},{1,33},{33,1},{2,34},{34,2},{3,35},{35,3},{4,36},{36... | collective-permute-start | bytes 786440 | tf_op jit(solution)/shard_map/ppermute | solution.py:217
  82.6 3.4 %collective-permute-start.2 = (bf16[8,128,128]{2,1,0:T(8,128)(2,1)S(1)}, bf16[8,128,128]{2,1,0:T(8,128)(2,1)S(1)}, u32[]{:S(2)}, u32[]{:S(2)}) collective-permute-start(bf16[8,128,128]{2,1,0:T(8,128)(2,1)S(1)} %collective-permute-done.refs_1_), channel_id=1, source_target_pairs={{0,32},{32,0},{1,33},{33,1},{2,34},{34,2},{3,35},{35,3},{4,36},{36... | collective-permute-start | bytes 786440 | tf_op jit(solution)/shard_map/ppermute | solution.py:217

commit v6 on v5

--- a/solution.py
+++ b/solution.py
@@ -131,9 +131,9 @@
     skip = jnp.concatenate([skip] * (block // LANES), axis=1)
     skip = jnp.concatenate([skip] * blocks, axis=0)
     gated = query.astype(jnp.float32) * (acc_ref[...] + skip * source.astype(jnp.float32))
-    gated = gated.astype(jnp.bfloat16).reshape(out_ref.shape[1:])
-    for i in range(out_ref.shape[0]):
-        out_ref[i] = gated
+    gated = gated.astype(jnp.bfloat16).reshape(out_ref.shape[:1] + out_ref.shape[2:])
+    for i in range(out_ref.shape[1]):
+        out_ref[:, i] = gated
 
 
 def convolve(pieces, filters, skip, count):
@@ -143,7 +143,7 @@
         conv_kernel,
         in_specs=[vmem(), vmem(), vmem()],
         out_specs=vmem(),
-        out_shape=jax.ShapeDtypeStruct((count, blocks, GROUP, block), jnp.bfloat16),
+        out_shape=jax.ShapeDtypeStruct((blocks, count, GROUP, block), jnp.bfloat16),
         scratch_shapes=[
             pltpu.VMEM((rows + GROUP, block), jnp.bfloat16),
             pltpu.VMEM((LANES, LANES + filters.shape[1]), jnp.bfloat16),
@@ -158,10 +158,10 @@
 def mix_kernel(g_ref, *refs):
     w_refs, out_ref, turned_ref = refs[:-2], refs[-2], refs[-1]
     core, odd = lax.axis_index("core"), lax.rem(lax.axis_index("z"), 2)
-    far, _, _, tokens = g_ref.shape
+    _, far, _, tokens = g_ref.shape
     peers, _, chans = w_refs[0].shape
     for i in range(far):
-        turned_ref[i] = g_ref[i].astype(jnp.float32).reshape(-1, tokens).T.astype(jnp.bfloat16)
+        turned_ref[i] = g_ref[:, i].astype(jnp.float32).reshape(-1, tokens).T.astype(jnp.bfloat16)
     acc = None
     for pair, at in ((w_refs[:2], core), (w_refs[2:], 1 - core)):
         left = jnp.concatenate([turned_ref[2 * at + odd], turned_ref[2 * at + 1 - odd]], axis=1)
@@ -175,7 +175,7 @@
 
 
 def mix(gated, *w):
-    far, groups, rows, tokens = gated.shape
+    groups, far, rows, tokens = gated.shape
     peers, _, chans = w[0].shape
     return pl.pallas_call(
         mix_kernel,
@@ -216,7 +216,7 @@
     gated = convolve(lax.all_gather(pieces, "core", axis=0), filters, skip.reshape(1, -1), 4)
     others = [lax.ppermute(rows, "core", [(0, 1), (1, 0)]) for rows in (own, beside)]
     shape = gated.shape
-    gated = lax.all_to_all(gated.reshape((-1,) + shape[2:]), ("y_far", "z"), 0, 0, tiled=True)
+    gated = lax.all_to_all(gated.reshape((-1,) + shape[2:]), ("z", "y_far"), 0, 0, tiled=True)
     parts = mix(gated.reshape(shape), own, beside, *others)
     return add(lax.all_to_all(parts, near, 0, 0, tiled=True))
 

time: 107 us -> 107 us (level); the launches traced: 106 us -> 107 us
  blocking collectives: 64 us -> 65.6 us
    all_to_all x1, blocking collectives: 12.1 us -> 13.6 us  [shards(): return add(lax.all_to_all(parts, near, 0, 0, tiled=True))]
where the time goes in v6:
time: 107 us
  blocking collectives  65.6 us (61%)
  starting transfers between devices  23.5 us (22%)
  waiting for transfers between devices  12.3 us (11%)
  Pallas kernels  5.56 us (5%)
    all_to_all x1, blocking collectives, shards(): x = lax.all_to_all(pack(x, w_out, 8), near, 0, 0, tiled=True)  28.7 us
    all_gather x1, blocking collectives, shards(): x = lax.all_gather(tokens, 'y_far', axis=0)  15.7 us
    all_to_all x1, blocking collectives, shards(): return add(lax.all_to_all(parts, near, 0, 0, tiled=True))  13.6 us
    all_to_all x1, starting transfers between devices, shards(): pieces = lax.all_to_all(pieces, 'z', 0, 0, tiled=True)  11.2 us
    all_gather x1, blocking collectives, shards(): lax.all_gather(pieces, 'core', axis=0)  7.61 us
    all_to_all x1, waiting for transfers between devices, shards(): lax.all_to_all(gated.reshape((-1,) + shape[2:]), ('z', 'y_far'), 0, 0, ti...  6.15 us
    all_to_all x1, waiting for transfers between devices, shards(): pieces = lax.all_to_all(pieces, 'z', 0, 0, tiled=True)  4.67 us
    ppermute x2, starting transfers between devices, shards(): lax.ppermute(rows, 'core', [(0, 1), (1, 0)])  4.46 us
  transfers between devices with their start and end apart: 5, of which 3 were waited for; matrix products, arithmetic and copies ran while one was open for 0% of the time, Pallas kernels for 1%

profile of v6, /device:TPU:1, one launch (start us, length us, event | category | flops | bytes accessed | tf_op | source)
XLA Modules:
  0.0 107.0 jit_solution(436292253926755274)
XLA Ops:
  0.0 15.7 %all-gather = bf16[1024,128]{1,0:T(8,128)(2,1)S(1)} all-gather(bf16[256,128]{1,0:T(8,128)(2,1)} %param.5), channel_id=2, replica_groups=mesh['z'=8,'core'=2,'x'=4,'y_far'=4,'y_near'=2] {'y_far'}, dimensions={0}, use_global_device_ids=true | all-gather | bytes 327680 | tf_op jit(solution)/shard_map/all_gather | solution.py:211
  15.7 1.0 pack.1
  16.6 0.0 copy-start
  16.7 28.7 %all_to_all.20.x_ref = bf16[8,1152,128]{2,1,0:T(8,128)(2,1)S(1)} all-to-all(bf16[8,1152,128]{2,1,0:T(8,128)(2,1)S(1)} %pack.1), channel_id=1, replica_groups=mesh['z'=8,'core'=2,'x'=4,'y_far'=4,'y_near'=2] {'x','y_near'}, dimensions={0} | all-to-all | bytes 4718592 | tf_op jit(solution)/shard_map/all_to_all | solution.py:212
  45.3 0.0 copy-done
  45.3 0.0 copy-start.1
  45.3 0.0 copy-start.2
  45.3 2.0 %project.1 = (bf16[8,32,256]{2,1,0:T(8,128)(2,1)}, bf16[8,128,128]{2,1,0:T(8,128)(2,1)S(1)}) custom-call(bf16[8,1152,128]{2,1,0:T(8,128)(2,1)S(1)} %all_to_all.20.x_ref, bf16[3,4096,128]{2,1,0:T(8,128)(2,1)S(1)} %bitcast.7), custom_call_target="tpu_custom_call" | custom-call | tf_op jit(solution)/shard_map/project/pallas_call | solution.py:78
  47.3 11.2 %all-to-all-start.1 = ((bf16[8,32,256]{2,1,0:T(8,128)(2,1)}), bf16[8,32,256]{2,1,0:T(8,128)(2,1)S(1)}, u32[]{:S(2)}, u32[]{:S(2)}) async-start(bf16[8,32,256]{2,1,0:T(8,128)(2,1)} %get-tuple-element.7), calls=%async_computation.1 | async-start | bytes 262144 | tf_op jit(solution)/shard_map/all_to_all | solution.py:215
  58.5 3.4 %collective-permute-start = (bf16[8,128,128]{2,1,0:T(8,128)(2,1)S(1)}, bf16[8,128,128]{2,1,0:T(8,128)(2,1)S(1)}, u32[]{:S(2)}, u32[]{:S(2)}) collective-permute-start(bf16[8,128,128]{2,1,0:T(8,128)(2,1)S(1)} %get-tuple-element.8.refs_0_), channel_id=1, source_target_pairs={{0,64},{64,0},{128,192},{192,128},{256,320},{320,256},{384,448},{4... | collective-permute-start | bytes 786440 | tf_op jit(solution)/shard_map/ppermute | solution.py:214
  61.9 4.7 %all-to-all-done.1 = bf16[8,32,256]{2,1,0:T(8,128)(2,1)S(1)} async-done(((bf16[8,32,256]{2,1,0:T(8,128)(2,1)}), bf16[8,32,256]{2,1,0:T(8,128)(2,1)S(1)}, u32[]{:S(2)}, u32[]{:S(2)}) %all-to-all-start.1) | async-done | bytes 131104 | tf_op jit(solution)/shard_map/all_to_all | solution.py:215
  66.6 7.6 %all-gather.1 = bf16[16,32,256]{2,1,0:T(8,128)(2,1)S(1)} all-gather(bf16[8,32,256]{2,1,0:T(8,128)(2,1)S(1)} %all-to-all-done.1), channel_id=3, replica_groups=mesh['z'=8,'core'=2,'x'=4,'y_far'=4,'y_near'=2] {'core'}, dimensions={0}, use_global_device_ids=true | all-gather | bytes 393216 | tf_op jit(solution)/shard_map/all_gather | solution.py:216
  74.2 0.0 copy-done.1
  74.2 0.0 copy-done.2
  74.2 1.4 %convolve.1 = bf16[8,4,16,256]{3,2,1,0:T(8,128)(2,1)} custom-call(bf16[2,8,32,256]{3,2,1,0:T(8,128)(2,1)S(1)} %bitcast.10, bf16[8,4096]{1,0:T(8,128)(2,1)S(1)} %copy-done.1, f32[1,128]{1,0:T(1,128)S(1)} %bitcast.11), custom_call_target="tpu_custom_call" | custom-call | tf_op jit(solution)/shard_map/convolve/pallas_call | solution.py:142
  75.6 4.4 %all-to-all-start.2 = ((bf16[32,16,256]{2,1,0:T(8,128)(2,1)}), bf16[32,16,256]{2,1,0:T(8,128)(2,1)S(1)}, u32[]{:S(2)}, u32[]{:S(2)}) async-start(bf16[32,16,256]{2,1,0:T(8,128)(2,1)} %bitcast.5), calls=%async_computation.2 | async-start | bytes 524288 | tf_op jit(solution)/shard_map/all_to_all | solution.py:219
  80.0 2.5 %collective-permute-start.1 = (bf16[8,128,128]{2,1,0:T(8,128)(2,1)S(1)}, bf16[8,128,128]{2,1,0:T(8,128)(2,1)S(1)}, u32[]{:S(2)}, u32[]{:S(2)}) collective-permute-start(bf16[8,128,128]{2,1,0:T(8,128)(2,1)S(1)} %get-tuple-element.8.refs_0_), channel_id=1, source_target_pairs={{0,32},{32,0},{1,33},{33,1},{2,34},{34,2},{3,35},{35,3},{4,36},{36... | collective-permute-start | bytes 786440 | tf_op jit(solution)/shard_map/ppermute | solution.py:217
  82.6 0.0 collective-permute-done.refs_1_
  82.6 1.9 %collective-permute-start.2 = (bf16[8,128,128]{2,1,0:T(8,128)(2,1)S(1)}, bf16[8,128,128]{2,1,0:T(8,128)(2,1)S(1)}, u32[]{:S(2)}, u32[]{:S(2)}) collective-permute-start(bf16[8,128,128]{2,1,0:T(8,128)(2,1)S(1)} %collective-permute-done.refs_1_), channel_id=1, source_target_pairs={{0,32},{32,0},{1,33},{33,1},{2,34},{34,2},{3,35},{35,3},{4,36},{36... | collective-permute-start | bytes 786440 | tf_op jit(solution)/shard_map/ppermute | solution.py:217
  84.5 0.0 collective-permute-done.1.refs_2_
  84.5 1.5 %collective-permute-done.2.refs_3_ = bf16[8,128,128]{2,1,0:T(8,128)(2,1)S(1)} collective-permute-done((bf16[8,128,128]{2,1,0:T(8,128)(2,1)S(1)}, bf16[8,128,128]{2,1,0:T(8,128)(2,1)S(1)}, u32[]{:S(2)}, u32[]{:S(2)}) %collective-permute-start.2) | collective-permute-done | bytes 262176 | tf_op jit(solution)/shard_map/ppermute | solution.py:217
  86.0 6.2 %all-to-all-done.2 = bf16[32,16,256]{2,1,0:T(8,128)(2,1)S(1)} async-done(((bf16[32,16,256]{2,1,0:T(8,128)(2,1)}), bf16[32,16,256]{2,1,0:T(8,128)(2,1)S(1)}, u32[]{:S(2)}, u32[]{:S(2)}) %all-to-all-start.2) | async-done | bytes 262176 | tf_op jit(solution)/shard_map/all_to_all | solution.py:219
  92.2 0.5 mix.1
  92.7 13.6 %all_to_all.21.parts_ref = bf16[8,256,128]{2,1,0:T(8,128)(2,1)S(1)} all-to-all(bf16[8,256,128]{2,1,0:T(8,128)(2,1)S(1)} %mix.1), channel_id=1, replica_groups=mesh['z'=8,'core'=2,'x'=4,'y_far'=4,'y_near'=2] {'x','y_near'}, dimensions={0} | all-to-all | bytes 1048576 | tf_op jit(solution)/shard_map/all_to_all | solution.py:221
  106.3 0.7 add.1
Async XLA Ops:
  16.6 28.7 %copy-start = (bf16[4096,3,128]{2,0,1:T(8,128)(2,1)S(1)}, bf16[4096,3,128]{2,0,1:T(8,128)(2,1)}, u32[]{:S(2)}) copy-start(bf16[4096,3,128]{2,0,1:T(8,128)(2,1)} %param.6) | copy-start | bytes 9437188
  45.3 28.9 %copy-start.1 = (bf16[8,4096]{1,0:T(8,128)(2,1)S(1)}, bf16[8,4096]{1,0:T(8,128)(2,1)}, u32[]{:S(2)}) copy-start(bf16[8,4096]{1,0:T(8,128)(2,1)} %filters_ref.1) | copy-start | bytes 196612
  45.3 28.9 %copy-start.2 = (f32[128]{0:T(128)S(1)}, f32[128]{0:T(128)}, u32[]{:S(2)}) copy-start(f32[128]{0:T(128)} %param.8) | copy-start | bytes 1540
  47.3 19.3 %all-to-all-start.1 = ((bf16[8,32,256]{2,1,0:T(8,128)(2,1)}), bf16[8,32,256]{2,1,0:T(8,128)(2,1)S(1)}, u32[]{:S(2)}, u32[]{:S(2)}) async-start(bf16[8,32,256]{2,1,0:T(8,128)(2,1)} %get-tuple-element.7), calls=%async_computation.1 | async-start | bytes 262144 | tf_op jit(solution)/shard_map/all_to_all | solution.py:215
  58.5 24.0 %collective-permute-start = (bf16[8,128,128]{2,1,0:T(8,128)(2,1)S(1)}, bf16[8,128,128]{2,1,0:T(8,128)(2,1)S(1)}, u32[]{:S(2)}, u32[]{:S(2)}) collective-permute-start(bf16[8,128,128]{2,1,0:T(8,128)(2,1)S(1)} %get-tuple-element.8.refs_0_), channel_id=1, source_target_pairs={{0,64},{64,0},{128,192},{192,128},{256,320},{320,256},{384,448},{4... | collective-permute-start | bytes 786440 | tf_op jit(solution)/shard_map/ppermute | solution.py:214
  75.6 16.6 %all-to-all-start.2 = ((bf16[32,16,256]{2,1,0:T(8,128)(2,1)}), bf16[32,16,256]{2,1,0:T(8,128)(2,1)S(1)}, u32[]{:S(2)}, u32[]{:S(2)}) async-start(bf16[32,16,256]{2,1,0:T(8,128)(2,1)} %bitcast.5), calls=%async_computation.2 | async-start | bytes 524288 | tf_op jit(solution)/shard_map/all_to_all | solution.py:219
  80.0 4.5 %collective-permute-start.1 = (bf16[8,128,128]{2,1,0:T(8,128)(2,1)S(1)}, bf16[8,128,128]{2,1,0:T(8,128)(2,1)S(1)}, u32[]{:S(2)}, u32[]{:S(2)}) collective-permute-start(bf16[8,128,128]{2,1,0:T(8,128)(2,1)S(1)} %get-tuple-element.8.refs_0_), channel_id=1, source_target_pairs={{0,32},{32,0},{1,33},{33,1},{2,34},{34,2},{3,35},{35,3},{4,36},{36... | collective-permute-start | bytes 786440 | tf_op jit(solution)/shard_map/ppermute | solution.py:217
  82.6 3.4 %collective-permute-start.2 = (bf16[8,128,128]{2,1,0:T(8,128)(2,1)S(1)}, bf16[8,128,128]{2,1,0:T(8,128)(2,1)S(1)}, u32[]{:S(2)}, u32[]{:S(2)}) collective-permute-start(bf16[8,128,128]{2,1,0:T(8,128)(2,1)S(1)} %collective-permute-done.refs_1_), channel_id=1, source_target_pairs={{0,32},{32,0},{1,33},{33,1},{2,34},{34,2},{3,35},{35,3},{4,36},{36... | collective-permute-start | bytes 786440 | tf_op jit(solution)/shard_map/ppermute | solution.py:217

commit v7 on v4

--- a/solution.py
+++ b/solution.py
@@ -15,26 +15,34 @@
     return pl.BlockSpec(*shape_and_map, memory_space=pltpu.VMEM)
 
 
-def pack_kernel(x_ref, w_ref, out_ref):
+def pack_kernel(x_ref, w_hbm, out_ref, sem):
     far, tokens, _ = x_ref.shape
-    depth = w_ref.shape[1]
+    steps, near, rows, _ = out_ref.shape
     mine = 2 * lax.axis_index("core") + lax.rem(lax.axis_index("z"), 2)
+    below = out_ref.at[:, :, pl.ds(far * tokens, rows - far * tokens)]
+    send = pltpu.make_async_copy(w_hbm.at[:, mine], below, sem)
+    send.start()
     x = x_ref[...].reshape(far * tokens, -1)
-    for peer in range(out_ref.shape[0]):
-        out_ref[peer, : far * tokens] = x
-        out_ref[peer, far * tokens :] = w_ref[(peer // 2 * far + mine) * 2 + peer % 2]
+    for step in range(steps):
+        for j in range(near):
+            out_ref[step, j, : far * tokens] = x
+    send.wait()
 
 
 def pack(x, w, peers):
     far, tokens, depth = x.shape
-    return pl.pallas_call(
+    chans = w.shape[1]
+    w = pltpu.with_memory_space_constraint(w.reshape(peers // 2, far, 2, depth, chans), pltpu.HBM)
+    packed = pl.pallas_call(
         pack_kernel,
-        in_specs=[vmem(), vmem()],
-        out_specs=vmem(),
-        out_shape=jax.ShapeDtypeStruct((peers, far * tokens + depth, depth), x.dtype),
+        in_specs=[vmem(), pl.BlockSpec(memory_space=pltpu.HBM)],
+        out_specs=vmem(),
+        out_shape=jax.ShapeDtypeStruct((peers // 2, 2, far * tokens + depth, depth), x.dtype),
+        scratch_shapes=[pltpu.SemaphoreType.DMA],
         compiler_params=PARAMS,
         name="pack",
-    )(x, w.reshape(-1, depth, w.shape[1]))
+    )(x, w)
+    return packed.reshape((peers,) + packed.shape[2:])
 
 
 def project_kernel(x_ref, w_ref, out_ref, rows_ref):

time: 107 us -> 107 us (level)
  local copies, waits for them, and re-layouts: 1.24 us -> 0.01 us
    unnamed x8 -> x6, local copies, waits for them, and re-layouts: 1.24 us -> 0.01 us
where the time goes in v7:
time: 107 us; the launch traced here: 106 us
  blocking collectives  64 us (60%)
  starting transfers between devices  23.5 us (22%)
  waiting for transfers between devices  12.5 us (12%)
  Pallas kernels  5.56 us (5%)
    all_to_all x1, blocking collectives, shards(): x = lax.all_to_all(pack(x, w_out, 8), near, 0, 0, tiled=True)  28.7 us
    all_gather x1, blocking collectives, shards(): x = lax.all_gather(tokens, 'y_far', axis=0)  15.7 us
    all_to_all x1, blocking collectives, shards(): return add(lax.all_to_all(parts, near, 0, 0, tiled=True))  12.1 us
    all_to_all x1, starting transfers between devices, shards(): pieces = lax.all_to_all(pieces, 'z', 0, 0, tiled=True)  11.2 us
    all_gather x1, blocking collectives, shards(): lax.all_gather(pieces, 'core', axis=0)  7.61 us
    all_to_all x1, waiting for transfers between devices, shards(): lax.all_to_all(gated.reshape((-1,) + shape[2:]), ('y_far', 'z'), 0, 0, ti...  6.33 us
    all_to_all x1, waiting for transfers between devices, shards(): pieces = lax.all_to_all(pieces, 'z', 0, 0, tiled=True)  4.67 us
    ppermute x2, starting transfers between devices, shards(): lax.ppermute(rows, 'core', [(0, 1), (1, 0)])  4.46 us
  transfers between devices with their start and end apart: 5, of which 3 were waited for; matrix products, arithmetic and copies ran while one was open for 0% of the time, Pallas kernels for 1%

profile of v7, /device:TPU:1, one launch (start us, length us, event | category | flops | bytes accessed | tf_op | source)
XLA Modules:
  0.0 105.7 jit_solution(5250032188391007820)
XLA Ops:
  0.0 15.7 %all-gather = bf16[1024,128]{1,0:T(8,128)(2,1)S(1)} all-gather(bf16[256,128]{1,0:T(8,128)(2,1)} %param.5), channel_id=2, replica_groups=mesh['z'=8,'core'=2,'x'=4,'y_far'=4,'y_near'=2] {'y_far'}, dimensions={0}, use_global_device_ids=true | all-gather | bytes 327680 | tf_op jit(solution)/shard_map/all_gather | solution.py:206
  15.7 1.0 pack.1
  16.6 0.0 copy-start
  16.7 28.7 %all_to_all.20.x_ref = bf16[8,1152,128]{2,1,0:T(8,128)(2,1)S(1)} all-to-all(bf16[8,1152,128]{2,1,0:T(8,128)(2,1)S(1)} %bitcast.8), channel_id=1, replica_groups=mesh['z'=8,'core'=2,'x'=4,'y_far'=4,'y_near'=2] {'x','y_near'}, dimensions={0} | all-to-all | bytes 4718592 | tf_op jit(solution)/shard_map/all_to_all | solution.py:207
  45.3 0.0 copy-done
  45.3 0.0 copy-start.1
  45.3 0.0 copy-start.2
  45.3 2.0 %project.1 = (bf16[8,32,256]{2,1,0:T(8,128)(2,1)}, bf16[8,128,128]{2,1,0:T(8,128)(2,1)S(1)}) custom-call(bf16[8,1152,128]{2,1,0:T(8,128)(2,1)S(1)} %all_to_all.20.x_ref, bf16[3,4096,128]{2,1,0:T(8,128)(2,1)S(1)} %bitcast.9), custom_call_target="tpu_custom_call" | custom-call | tf_op jit(solution)/shard_map/project/pallas_call | solution.py:73
  47.3 11.2 %all-to-all-start.1 = ((bf16[8,32,256]{2,1,0:T(8,128)(2,1)}), bf16[8,32,256]{2,1,0:T(8,128)(2,1)S(1)}, u32[]{:S(2)}, u32[]{:S(2)}) async-start(bf16[8,32,256]{2,1,0:T(8,128)(2,1)} %get-tuple-element.7), calls=%async_computation.1 | async-start | bytes 262144 | tf_op jit(solution)/shard_map/all_to_all | solution.py:210
  58.6 3.4 %collective-permute-start = (bf16[8,128,128]{2,1,0:T(8,128)(2,1)S(1)}, bf16[8,128,128]{2,1,0:T(8,128)(2,1)S(1)}, u32[]{:S(2)}, u32[]{:S(2)}) collective-permute-start(bf16[8,128,128]{2,1,0:T(8,128)(2,1)S(1)} %get-tuple-element.8.refs_0_), channel_id=1, source_target_pairs={{0,64},{64,0},{128,192},{192,128},{256,320},{320,256},{384,448},{4... | collective-permute-start | bytes 786440 | tf_op jit(solution)/shard_map/ppermute | solution.py:209
  61.9 4.7 %all-to-all-done.1 = bf16[8,32,256]{2,1,0:T(8,128)(2,1)S(1)} async-done(((bf16[8,32,256]{2,1,0:T(8,128)(2,1)}), bf16[8,32,256]{2,1,0:T(8,128)(2,1)S(1)}, u32[]{:S(2)}, u32[]{:S(2)}) %all-to-all-start.1) | async-done | bytes 131104 | tf_op jit(solution)/shard_map/all_to_all | solution.py:210
  66.6 7.6 %all-gather.1 = bf16[16,32,256]{2,1,0:T(8,128)(2,1)S(1)} all-gather(bf16[8,32,256]{2,1,0:T(8,128)(2,1)S(1)} %all-to-all-done.1), channel_id=3, replica_groups=mesh['z'=8,'core'=2,'x'=4,'y_far'=4,'y_near'=2] {'core'}, dimensions={0}, use_global_device_ids=true | all-gather | bytes 393216 | tf_op jit(solution)/shard_map/all_gather | solution.py:211
  74.2 0.0 copy-done.1
  74.2 0.0 copy-done.2
  74.2 1.4 %convolve.1 = bf16[4,8,16,256]{3,2,1,0:T(8,128)(2,1)} custom-call(bf16[2,8,32,256]{3,2,1,0:T(8,128)(2,1)S(1)} %bitcast.12, bf16[8,4096]{1,0:T(8,128)(2,1)S(1)} %copy-done.1, f32[1,128]{1,0:T(1,128)S(1)} %bitcast.13), custom_call_target="tpu_custom_call" | custom-call | tf_op jit(solution)/shard_map/convolve/pallas_call | solution.py:137
  75.6 4.4 %all-to-all-start.2 = ((bf16[32,16,256]{2,1,0:T(8,128)(2,1)}), bf16[32,16,256]{2,1,0:T(8,128)(2,1)S(1)}, u32[]{:S(2)}, u32[]{:S(2)}) async-start(bf16[32,16,256]{2,1,0:T(8,128)(2,1)} %bitcast.6), calls=%async_computation.2 | async-start | bytes 524288 | tf_op jit(solution)/shard_map/all_to_all | solution.py:214
  80.0 2.5 %collective-permute-start.1 = (bf16[8,128,128]{2,1,0:T(8,128)(2,1)S(1)}, bf16[8,128,128]{2,1,0:T(8,128)(2,1)S(1)}, u32[]{:S(2)}, u32[]{:S(2)}) collective-permute-start(bf16[8,128,128]{2,1,0:T(8,128)(2,1)S(1)} %get-tuple-element.8.refs_0_), channel_id=1, source_target_pairs={{0,32},{32,0},{1,33},{33,1},{2,34},{34,2},{3,35},{35,3},{4,36},{36... | collective-permute-start | bytes 786440 | tf_op jit(solution)/shard_map/ppermute | solution.py:212
  82.6 0.0 collective-permute-done.refs_1_
  82.6 1.9 %collective-permute-start.2 = (bf16[8,128,128]{2,1,0:T(8,128)(2,1)S(1)}, bf16[8,128,128]{2,1,0:T(8,128)(2,1)S(1)}, u32[]{:S(2)}, u32[]{:S(2)}) collective-permute-start(bf16[8,128,128]{2,1,0:T(8,128)(2,1)S(1)} %collective-permute-done.refs_1_), channel_id=1, source_target_pairs={{0,32},{32,0},{1,33},{33,1},{2,34},{34,2},{3,35},{35,3},{4,36},{36... | collective-permute-start | bytes 786440 | tf_op jit(solution)/shard_map/ppermute | solution.py:212
  84.5 0.0 collective-permute-done.1.refs_2_
  84.5 1.5 %collective-permute-done.2.refs_3_ = bf16[8,128,128]{2,1,0:T(8,128)(2,1)S(1)} collective-permute-done((bf16[8,128,128]{2,1,0:T(8,128)(2,1)S(1)}, bf16[8,128,128]{2,1,0:T(8,128)(2,1)S(1)}, u32[]{:S(2)}, u32[]{:S(2)}) %collective-permute-start.2) | collective-permute-done | bytes 262176 | tf_op jit(solution)/shard_map/ppermute | solution.py:212
  86.0 6.3 %all-to-all-done.2 = bf16[32,16,256]{2,1,0:T(8,128)(2,1)S(1)} async-done(((bf16[32,16,256]{2,1,0:T(8,128)(2,1)}), bf16[32,16,256]{2,1,0:T(8,128)(2,1)S(1)}, u32[]{:S(2)}, u32[]{:S(2)}) %all-to-all-start.2) | async-done | bytes 262176 | tf_op jit(solution)/shard_map/all_to_all | solution.py:214
  92.3 0.5 mix.1
  92.9 12.1 %all_to_all.21.parts_ref = bf16[8,256,128]{2,1,0:T(8,128)(2,1)S(1)} all-to-all(bf16[8,256,128]{2,1,0:T(8,128)(2,1)S(1)} %mix.1), channel_id=1, replica_groups=mesh['z'=8,'core'=2,'x'=4,'y_far'=4,'y_near'=2] {'x','y_near'}, dimensions={0} | all-to-all | bytes 1048576 | tf_op jit(solution)/shard_map/all_to_all | solution.py:216
  105.0 0.7 add.1
Async XLA Ops:
  16.6 28.7 %copy-start = (bf16[4096,3,128]{2,0,1:T(8,128)(2,1)S(1)}, bf16[4096,3,128]{2,0,1:T(8,128)(2,1)}, u32[]{:S(2)}) copy-start(bf16[4096,3,128]{2,0,1:T(8,128)(2,1)} %param.6) | copy-start | bytes 9437188
  45.3 28.9 %copy-start.1 = (bf16[8,4096]{1,0:T(8,128)(2,1)S(1)}, bf16[8,4096]{1,0:T(8,128)(2,1)}, u32[]{:S(2)}) copy-start(bf16[8,4096]{1,0:T(8,128)(2,1)} %filters_ref.1) | copy-start | bytes 196612
  45.3 28.9 %copy-start.2 = (f32[128]{0:T(128)S(1)}, f32[128]{0:T(128)}, u32[]{:S(2)}) copy-start(f32[128]{0:T(128)} %param.8) | copy-start | bytes 1540
  47.3 19.3 %all-to-all-start.1 = ((bf16[8,32,256]{2,1,0:T(8,128)(2,1)}), bf16[8,32,256]{2,1,0:T(8,128)(2,1)S(1)}, u32[]{:S(2)}, u32[]{:S(2)}) async-start(bf16[8,32,256]{2,1,0:T(8,128)(2,1)} %get-tuple-element.7), calls=%async_computation.1 | async-start | bytes 262144 | tf_op jit(solution)/shard_map/all_to_all | solution.py:210
  58.6 24.0 %collective-permute-start = (bf16[8,128,128]{2,1,0:T(8,128)(2,1)S(1)}, bf16[8,128,128]{2,1,0:T(8,128)(2,1)S(1)}, u32[]{:S(2)}, u32[]{:S(2)}) collective-permute-start(bf16[8,128,128]{2,1,0:T(8,128)(2,1)S(1)} %get-tuple-element.8.refs_0_), channel_id=1, source_target_pairs={{0,64},{64,0},{128,192},{192,128},{256,320},{320,256},{384,448},{4... | collective-permute-start | bytes 786440 | tf_op jit(solution)/shard_map/ppermute | solution.py:209
  75.6 16.8 %all-to-all-start.2 = ((bf16[32,16,256]{2,1,0:T(8,128)(2,1)}), bf16[32,16,256]{2,1,0:T(8,128)(2,1)S(1)}, u32[]{:S(2)}, u32[]{:S(2)}) async-start(bf16[32,16,256]{2,1,0:T(8,128)(2,1)} %bitcast.6), calls=%async_computation.2 | async-start | bytes 524288 | tf_op jit(solution)/shard_map/all_to_all | solution.py:214
  80.0 4.5 %collective-permute-start.1 = (bf16[8,128,128]{2,1,0:T(8,128)(2,1)S(1)}, bf16[8,128,128]{2,1,0:T(8,128)(2,1)S(1)}, u32[]{:S(2)}, u32[]{:S(2)}) collective-permute-start(bf16[8,128,128]{2,1,0:T(8,128)(2,1)S(1)} %get-tuple-element.8.refs_0_), channel_id=1, source_target_pairs={{0,32},{32,0},{1,33},{33,1},{2,34},{34,2},{3,35},{35,3},{4,36},{36... | collective-permute-start | bytes 786440 | tf_op jit(solution)/shard_map/ppermute | solution.py:212
  82.6 3.4 %collective-permute-start.2 = (bf16[8,128,128]{2,1,0:T(8,128)(2,1)S(1)}, bf16[8,128,128]{2,1,0:T(8,128)(2,1)S(1)}, u32[]{:S(2)}, u32[]{:S(2)}) collective-permute-start(bf16[8,128,128]{2,1,0:T(8,128)(2,1)S(1)} %collective-permute-done.refs_1_), channel_id=1, source_target_pairs={{0,32},{32,0},{1,33},{33,1},{2,34},{34,2},{3,35},{35,3},{4,36},{36... | collective-permute-start | bytes 786440 | tf_op jit(solution)/shard_map/ppermute | solution.py:212
